TPU v7x, 32 devices: a whole 2x2x4 slice. The times are simulated.
32 devices in a mesh: dp: 8 (over y, x, core), mp: 4 (over z).
Axes of the slice: x: 2, y: 2, z: 4, core: 2. Of those that a mesh axis runs over, the one named last changes fastest.
Arguments:
- tokens: bfloat16 [8, 1024, 768], P('dp', 'mp'), may hold values from -6 to 6
- cotangent: bfloat16 [8, 1024, 768], P('dp', 'mp'), may hold values from -6 to 6
- first_gain: bfloat16 [768], P('dp'), may hold values from 0.099609375 to 1.8984375
- first_shift: bfloat16 [768], P('dp'), may hold values from -3 to 3
- w_query: bfloat16 [768, 768], P('dp', 'mp'), may hold values from -0.21875 to 0.21875
- b_query: bfloat16 [12, 64], P('mp', 'dp'), may hold values from -3 to 3
- w_key: bfloat16 [768, 768], P('dp', 'mp'), may hold values from -0.21875 to 0.21875
- w_value: bfloat16 [768, 768], P('dp', 'mp'), may hold values from -0.21875 to 0.21875
- b_value: bfloat16 [12, 64], P('mp', 'dp'), may hold values from -3 to 3
- w_out: bfloat16 [768, 768], P('mp', 'dp'), may hold values from -0.625 to 0.625
- b_out: bfloat16 [768], P('dp'), may hold values from -3 to 3
- second_gain: bfloat16 [768], P('dp'), may hold values from 0.099609375 to 1.8984375
- second_shift: bfloat16 [768], P('dp'), may hold values from -3 to 3
- w_expand: bfloat16 [768, 3072], P('dp', 'mp'), may hold values from -0.21875 to 0.21875
- b_expand: bfloat16 [48, 64], P('mp', 'dp'), may hold values from -3 to 3
- w_reduce: bfloat16 [3072, 768], P('mp', 'dp'), may hold values from -0.15625 to 0.15625
- b_reduce: bfloat16 [768], P('dp'), may hold values from -3 to 3
Outputs:
- result: bfloat16 [8, 1024, 768], P('dp', 'mp')
- grad_tokens: float32 [8, 1024, 768], P('dp', 'mp')
- grad_first_gain: float32 [768], P('dp')
- grad_first_shift: float32 [768], P('dp')
- grad_w_query: float32 [768, 768], P('dp', 'mp')
- grad_b_query: float32 [12, 64], P('mp', 'dp')
- grad_w_key: float32 [768, 768], P('dp', 'mp')
- grad_w_value: float32 [768, 768], P('dp', 'mp')
- grad_b_value: float32 [12, 64], P('mp', 'dp')
- grad_w_out: float32 [768, 768], P('mp', 'dp')
- grad_b_out: float32 [768], P('dp')
- grad_second_gain: float32 [768], P('dp')
- grad_second_shift: float32 [768], P('dp')
- grad_w_expand: float32 [768, 3072], P('dp', 'mp')
- grad_b_expand: float32 [48, 64], P('mp', 'dp')
- grad_w_reduce: float32 [3072, 768], P('mp', 'dp')
- grad_b_reduce: float32 [768], P('dp')
All inputs are finite; a program needn't handle non-finite values.
Results may differ from a plain program's by a relative error of at most 0.019.
Values may be sent and summed in bfloat16 or wider, within the bound.
A program may use at most 128 MiB of HBM per device.

v0:
```python
import jax
import jax.numpy as jnp
from jax import lax
from jax.sharding import PartitionSpec as P

HD = 64


def norm_rows(v, gain, shift):
    mean = jnp.mean(v, axis=-1, keepdims=True)
    centered = v - mean
    spread = jnp.mean(centered * centered, axis=-1, keepdims=True)
    return centered * lax.rsqrt(spread + 1e-05) * gain + shift


def gelu_tanh(v):
    return 0.5 * v * (1.0 + jnp.tanh(0.7978845608028654 * (v + 0.044715 * v * v * v)))


def gather_rows(v):
    return lax.all_gather(v, "mp", axis=1, tiled=True)


def scatter_rows(v):
    return lax.psum_scatter(v.astype(jnp.bfloat16), "mp", scatter_dimension=1, tiled=True).astype(
        jnp.float32
    )


def block_scores(qhead, khead, first, end, scale):
    scores = (
        jnp.einsum(
            "qhd,khd->hqk", qhead[first:end], khead[:end], preferred_element_type=jnp.float32
        )
        * scale
    )
    causal = (first + jnp.arange(end - first))[:, None] >= jnp.arange(end)[None, :]
    return jnp.where(causal[None], scores, -1e30)


def attend_forward(query, keys, values, heads):
    length = query.shape[0]
    block = min(512, length)
    scale = HD ** (-0.5)
    qhead = query.reshape(length, heads, HD)
    khead = keys.reshape(length, heads, HD)
    vhead = values.reshape(length, heads, HD)
    pieces, maxima, totals = ([], [], [])
    for first in range(0, length, block):
        end = first + block
        scores = block_scores(qhead, khead, first, end, scale)
        top = jnp.max(scores, axis=-1, keepdims=True)
        expo = jnp.exp(scores - top)
        total = jnp.sum(expo, axis=-1, keepdims=True)
        probs = (expo / total).astype(jnp.bfloat16)
        mixed = jnp.einsum("hqk,khd->qhd", probs, vhead[:end], preferred_element_type=jnp.float32)
        pieces.append(mixed.reshape(block, heads * HD).astype(jnp.bfloat16))
        maxima.append(top)
        totals.append(total)
    return (jnp.concatenate(pieces, 0), maxima, totals)


def attend_backward(query, keys, values, d_mixed, maxima, totals, heads):
    length = query.shape[0]
    block = min(512, length)
    scale = HD ** (-0.5)
    qhead = query.reshape(length, heads, HD)
    khead = keys.reshape(length, heads, HD)
    vhead = values.reshape(length, heads, HD)
    dhead = d_mixed.reshape(length, heads, HD)
    key_acc = jnp.zeros((length, heads, HD), jnp.float32)
    value_acc = jnp.zeros((length, heads, HD), jnp.float32)
    query_parts = []
    for number, first in enumerate(range(0, length, block)):
        end = first + block
        scores = block_scores(qhead, khead, first, end, scale)
        probs = jnp.exp(scores - maxima[number]) / totals[number]
        d_probs = jnp.einsum(
            "qhd,khd->hqk", dhead[first:end], vhead[:end], preferred_element_type=jnp.float32
        )
        inner = jnp.sum(probs * d_probs, axis=-1, keepdims=True)
        d_scores = (probs * (d_probs - inner)).astype(jnp.bfloat16)
        d_query = (
            jnp.einsum("hqk,khd->qhd", d_scores, khead[:end], preferred_element_type=jnp.float32)
            * scale
        )
        query_parts.append(d_query.reshape(block, heads * HD).astype(jnp.bfloat16))
        key_acc = key_acc.at[:end].add(
            jnp.einsum(
                "hqk,qhd->khd", d_scores, qhead[first:end], preferred_element_type=jnp.float32
            )
            * scale
        )
        value_acc = value_acc.at[:end].add(
            jnp.einsum(
                "hqk,qhd->khd",
                probs.astype(jnp.bfloat16),
                dhead[first:end],
                preferred_element_type=jnp.float32,
            )
        )
    d_keys = key_acc.reshape(length, heads * HD).astype(jnp.bfloat16)
    d_values = value_acc.reshape(length, heads * HD).astype(jnp.bfloat16)
    return (jnp.concatenate(query_parts, 0), d_keys, d_values)


def local(
    tokens,
    cotangent,
    first_gain,
    first_shift,
    w_query,
    b_query,
    w_key,
    w_value,
    b_value,
    w_out,
    b_out,
    second_gain,
    second_shift,
    w_expand,
    b_expand,
    w_reduce,
    b_reduce,
):
    attn_set = (
        lax.all_gather(first_gain, "dp", axis=0, tiled=True),
        lax.all_gather(first_shift, "dp", axis=0, tiled=True),
        lax.all_gather(w_query, "dp", axis=0, tiled=True),
        lax.all_gather(b_query, "dp", axis=1, tiled=True),
        lax.all_gather(w_key, "dp", axis=0, tiled=True),
        lax.all_gather(w_value, "dp", axis=0, tiled=True),
        lax.all_gather(b_value, "dp", axis=1, tiled=True),
        lax.all_gather(w_out, "dp", axis=1, tiled=True),
        lax.all_gather(b_out, "dp", axis=0, tiled=True),
    )
    shard = tokens.astype(jnp.float32)
    seqs, local_len, width = shard.shape
    normed_one, back_first = jax.vjp(
        norm_rows, shard, attn_set[0].astype(jnp.float32), attn_set[1].astype(jnp.float32)
    )
    inputs_one = gather_rows(normed_one.astype(jnp.bfloat16))
    length = inputs_one.shape[1]
    rows_one = inputs_one.reshape(seqs * length, width)
    query = (
        jnp.dot(rows_one, attn_set[2], preferred_element_type=jnp.float32)
        + attn_set[3].reshape(-1).astype(jnp.float32)
    ).astype(jnp.bfloat16)
    keys = jnp.dot(rows_one, attn_set[4], preferred_element_type=jnp.float32).astype(jnp.bfloat16)
    values = (
        jnp.dot(rows_one, attn_set[5], preferred_element_type=jnp.float32)
        + attn_set[6].reshape(-1).astype(jnp.float32)
    ).astype(jnp.bfloat16)
    heads_here = query.shape[1] // HD
    mixed_parts, kept_stats = ([], [])
    part, maxima, totals = attend_forward(query, keys, values, heads_here)
    mixed_parts.append(part)
    kept_stats.append((maxima, totals))
    mixed = mixed_parts[0]
    mlp_set = (
        lax.all_gather(second_gain, "dp", axis=0, tiled=True),
        lax.all_gather(second_shift, "dp", axis=0, tiled=True),
        lax.all_gather(w_expand, "dp", axis=0, tiled=True),
        lax.all_gather(b_expand, "dp", axis=1, tiled=True),
        lax.all_gather(w_reduce, "dp", axis=1, tiled=True),
        lax.all_gather(b_reduce, "dp", axis=0, tiled=True),
    )
    partial_one = jnp.dot(mixed, attn_set[7], preferred_element_type=jnp.float32).reshape(
        seqs, length, width
    )
    gain_two = mlp_set[0].astype(jnp.float32)
    shift_two = mlp_set[1].astype(jnp.float32)
    hidden = shard + scatter_rows(partial_one) + attn_set[8].astype(jnp.float32)
    normed_two, back_second = jax.vjp(norm_rows, hidden, gain_two, shift_two)
    inputs_two = gather_rows(normed_two.astype(jnp.bfloat16))
    rows_two = inputs_two.reshape(seqs * length, width)
    pre = jnp.dot(rows_two, mlp_set[2], preferred_element_type=jnp.float32) + mlp_set[3].reshape(
        -1
    ).astype(jnp.float32)
    act_full, back_gelu = jax.vjp(gelu_tanh, pre)
    act = act_full.astype(jnp.bfloat16)
    partial_two = jnp.dot(act, mlp_set[4], preferred_element_type=jnp.float32).reshape(
        seqs, length, width
    )
    result = (hidden + scatter_rows(partial_two) + mlp_set[5].astype(jnp.float32)).astype(
        jnp.bfloat16
    )
    mlp_back = (
        lax.all_gather(second_gain, "dp", axis=0, tiled=True),
        lax.all_gather(second_shift, "dp", axis=0, tiled=True),
        lax.all_gather(w_expand, "dp", axis=0, tiled=True),
        lax.all_gather(b_expand, "dp", axis=1, tiled=True),
        lax.all_gather(w_reduce, "dp", axis=1, tiled=True),
        lax.all_gather(b_reduce, "dp", axis=0, tiled=True),
    )
    grad_out = cotangent.astype(jnp.float32)
    out_full = gather_rows(cotangent)
    out_rows = out_full.reshape(seqs * length, width)
    grad_reduce = jnp.einsum("rf,rd->fd", act, out_rows, preferred_element_type=jnp.float32)
    grad_breduce = jnp.sum(grad_out, axis=(0, 1))
    d_act = jnp.einsum("rd,fd->rf", out_rows, mlp_back[4], preferred_element_type=jnp.float32)
    (d_pre_full,) = back_gelu(d_act)
    d_pre = d_pre_full.astype(jnp.bfloat16)
    grad_expand = jnp.einsum("rd,rf->df", rows_two, d_pre, preferred_element_type=jnp.float32)
    grad_bexpand = jnp.sum(d_pre.astype(jnp.float32), axis=0).reshape(-1, HD)
    d_second_part = jnp.einsum("rf,df->rd", d_pre, mlp_back[2], preferred_element_type=jnp.float32)
    d_second = scatter_rows(d_second_part.reshape(seqs, length, width))
    d_hidden_norm, grad_gain_two, grad_shift_two = back_second(d_second)
    d_hidden = grad_out + d_hidden_norm
    d_hidden_low = d_hidden.astype(jnp.bfloat16)
    hidden_rows = gather_rows(d_hidden_low).reshape(seqs * length, width)
    grad_bout = jnp.sum(d_hidden_low.astype(jnp.float32), axis=(0, 1))
    attn_back = (
        lax.all_gather(first_gain, "dp", axis=0, tiled=True),
        lax.all_gather(first_shift, "dp", axis=0, tiled=True),
        lax.all_gather(w_query, "dp", axis=0, tiled=True),
        lax.all_gather(b_query, "dp", axis=1, tiled=True),
        lax.all_gather(w_key, "dp", axis=0, tiled=True),
        lax.all_gather(w_value, "dp", axis=0, tiled=True),
        lax.all_gather(b_value, "dp", axis=1, tiled=True),
        lax.all_gather(w_out, "dp", axis=1, tiled=True),
        lax.all_gather(b_out, "dp", axis=0, tiled=True),
    )
    grad_out_proj = jnp.einsum("re,rd->ed", mixed, hidden_rows, preferred_element_type=jnp.float32)
    d_mixed = jnp.einsum(
        "rd,ed->re", hidden_rows, attn_back[7], preferred_element_type=jnp.float32
    ).astype(jnp.bfloat16)
    query_grads, key_grads, value_grads = ([], [], [])
    maxima, totals = kept_stats[0]
    d_query, d_keys, d_values = attend_backward(
        query, keys, values, d_mixed, maxima, totals, heads_here
    )
    query_grads.append(d_query)
    key_grads.append(d_keys)
    value_grads.append(d_values)
    d_query = query_grads[0]
    d_keys = key_grads[0]
    d_values = value_grads[0]
    grad_query = jnp.einsum("rd,re->de", rows_one, d_query, preferred_element_type=jnp.float32)
    grad_key = jnp.einsum("rd,re->de", rows_one, d_keys, preferred_element_type=jnp.float32)
    grad_value = jnp.einsum("rd,re->de", rows_one, d_values, preferred_element_type=jnp.float32)
    grad_bquery = jnp.sum(d_query.astype(jnp.float32), axis=0).reshape(-1, HD)
    grad_bvalue = jnp.sum(d_values.astype(jnp.float32), axis=0).reshape(-1, HD)
    d_first_part = (
        jnp.einsum("re,de->rd", d_query, attn_back[2], preferred_element_type=jnp.float32)
        + jnp.einsum("re,de->rd", d_keys, attn_back[4], preferred_element_type=jnp.float32)
        + jnp.einsum("re,de->rd", d_values, attn_back[5], preferred_element_type=jnp.float32)
    )
    d_first = scatter_rows(d_first_part.reshape(seqs, length, width))
    d_input_norm, grad_gain_one, grad_shift_one = back_first(d_first)
    grad_tokens = d_hidden + d_input_norm
    owned = (
        lax.psum_scatter(grad_gain_one, "dp", scatter_dimension=0, tiled=True),
        lax.psum_scatter(grad_shift_one, "dp", scatter_dimension=0, tiled=True),
        lax.psum_scatter(grad_query, "dp", scatter_dimension=0, tiled=True),
        lax.psum_scatter(grad_bquery, "dp", scatter_dimension=1, tiled=True),
        lax.psum_scatter(grad_key, "dp", scatter_dimension=0, tiled=True),
        lax.psum_scatter(grad_value, "dp", scatter_dimension=0, tiled=True),
        lax.psum_scatter(grad_bvalue, "dp", scatter_dimension=1, tiled=True),
        lax.psum_scatter(grad_out_proj, "dp", scatter_dimension=1, tiled=True),
        lax.psum_scatter(grad_bout, "dp", scatter_dimension=0, tiled=True),
        lax.psum_scatter(grad_expand, "dp", scatter_dimension=0, tiled=True),
        lax.psum_scatter(grad_bexpand, "dp", scatter_dimension=1, tiled=True),
        lax.psum_scatter(grad_reduce, "dp", scatter_dimension=1, tiled=True),
        lax.psum_scatter(grad_gain_two, "dp", scatter_dimension=0, tiled=True),
        lax.psum_scatter(grad_shift_two, "dp", scatter_dimension=0, tiled=True),
        lax.psum_scatter(grad_breduce, "dp", scatter_dimension=0, tiled=True),
    )
    vectors = lax.psum((owned[0], owned[1], owned[8], owned[12], owned[13], owned[14]), "mp")
    return (
        result,
        grad_tokens,
        vectors[0],
        vectors[1],
        owned[2],
        owned[3],
        owned[4],
        owned[5],
        owned[6],
        owned[7],
        vectors[2],
        vectors[3],
        vectors[4],
        owned[9],
        owned[10],
        owned[11],
        vectors[5],
    )


def solution(mesh):
    return jax.shard_map(
        local,
        mesh=mesh,
        in_specs=(
            P("dp", "mp", None),
            P("dp", "mp", None),
            P("dp"),
            P("dp"),
            P("dp", "mp"),
            P("mp", "dp"),
            P("dp", "mp"),
            P("dp", "mp"),
            P("mp", "dp"),
            P("mp", "dp"),
            P("dp"),
            P("dp"),
            P("dp"),
            P("dp", "mp"),
            P("mp", "dp"),
            P("mp", "dp"),
            P("dp"),
        ),
        out_specs=(
            P("dp", "mp", None),
            P("dp", "mp", None),
            P("dp"),
            P("dp"),
            P("dp", "mp"),
            P("mp", "dp"),
            P("dp", "mp"),
            P("dp", "mp"),
            P("mp", "dp"),
            P("mp", "dp"),
            P("dp"),
            P("dp"),
            P("dp"),
            P("dp", "mp"),
            P("mp", "dp"),
            P("mp", "dp"),
            P("dp"),
        ),
        check_vma=False,
    )
```

profile of v0, /device:TPU:0, one launch (start us, length us, event | category | flops | bytes accessed | tf_op | source)
XLA Modules:
  0.0 687.6 jit_solution(2174843435618049507)
XLA Ops:
  17.5 25.5 %all-reduce.19 = (bf16[768]{0:T(1024)(128)(2,1)}, bf16[768]{0:T(1024)(128)(2,1)}, bf16[768]{0:T(1024)(128)(2,1)S(1)}, bf16[768]{0:T(1024)(128)(2,1)S(1)}, bf16[768]{0:T(1024)(128)(2,1)}, /*index=5*/bf16[768]{0:T(1024)(128)(2,1)}) all-reduce(bf16[768]{0:T(1024)(128)(2,1)S(1)} %dynamic-update-slice.14, ...), channel_id=1, replica_groups=mesh['dp'=8,'mp'=4] {'dp'}, use_global_device_ids=true, to_apply=%add.6 | all-reduce | flops 4608 | bytes 18432
  45.1 8.5 %all-gather.1 = bf16[8,8,3]{1,2,0:T(4,128)(2,1)S(1)} all-gather(bf16[1,8,3]{1,2,0:T(4,128)(2,1)} %bitcast.190), channel_id=1, replica_groups=mesh['dp'=8,'mp'=4] {'dp'}, dimensions={0}, use_global_device_ids=true | all-gather | bytes 432 | tf_op jit(solution)/shard_map/all_gather | solution.py:130
  54.3 8.3 %all-gather = bf16[8,8,3]{1,2,0:T(4,128)(2,1)S(1)} all-gather(bf16[1,8,3]{1,2,0:T(4,128)(2,1)} %bitcast.191), channel_id=1, replica_groups=mesh['dp'=8,'mp'=4] {'dp'}, dimensions={0}, use_global_device_ids=true | all-gather | bytes 432 | tf_op jit(solution)/shard_map/all_gather | solution.py:133
  64.3 9.1 %all_gather.71 = bf16[192,768]{0,1:T(8,128)(2,1)S(1)} all-gather(bf16[192,96]{0,1:T(8,128)(2,1)S(1)} %copy.67), channel_id=1, replica_groups=mesh['dp'=8,'mp'=4] {'dp'}, dimensions={1}, use_global_device_ids=true | all-gather | bytes 331776 | tf_op jit(solution)/shard_map/all_gather | solution.py:134
  73.4 9.0 %all_gather.68 = bf16[768,192]{1,0:T(8,128)(2,1)S(1)} all-gather(bf16[96,192]{1,0:T(8,128)(2,1)} %param.33), channel_id=1, replica_groups=mesh['dp'=8,'mp'=4] {'dp'}, dimensions={0}, use_global_device_ids=true | all-gather | bytes 331776 | tf_op jit(solution)/shard_map/all_gather | solution.py:129
  82.4 9.1 %all_gather.70 = bf16[768,192]{1,0:T(8,128)(2,1)S(1)} all-gather(bf16[96,192]{1,0:T(8,128)(2,1)S(1)} %copy-done.32), channel_id=1, replica_groups=mesh['dp'=8,'mp'=4] {'dp'}, dimensions={0}, use_global_device_ids=true | all-gather | bytes 331776 | tf_op jit(solution)/shard_map/all_gather | solution.py:131
  91.6 9.5 %all_gather.66 = bf16[768,192]{1,0:T(8,128)(2,1)S(1)} all-gather(bf16[96,192]{1,0:T(8,128)(2,1)S(1)} %copy-done.33), channel_id=1, replica_groups=mesh['dp'=8,'mp'=4] {'dp'}, dimensions={0}, use_global_device_ids=true | all-gather | bytes 331776 | tf_op jit(solution)/shard_map/all_gather | solution.py:132
  108.2 4.9 fusion.132
  116.1 6.0 fusion.131
  122.7 4.0 fusion.90
  129.3 35.1 %reduce-scatter.16.cloned.1.call-done = bf16[1,256,768]{2,1,0:T(8,128)(2,1)} async-done(((bf16[1,1024,768]{2,1,0:T(8,128)(2,1)}), bf16[1,256,768]{2,1,0:T(8,128)(2,1)}) %reduce-scatter.16.cloned.1.call-update) | async-done | bytes 393232 | tf_op jit(solution)/shard_map/reduce_scatter | solution.py:25
  170.2 9.0 %all_gather.77 = bf16[12,64]{0,1:T(8,128)(2,1)S(1)} all-gather(bf16[12,8]{0,1:T(8,128)(2,1)S(1)} %copy-done.52), channel_id=1, replica_groups=mesh['dp'=8,'mp'=4] {'dp'}, dimensions={1}, use_global_device_ids=true | all-gather | bytes 1728 | tf_op jit(solution)/shard_map/all_gather | solution.py:164
  179.4 25.5 %all-gather.11.cloned.1.call-done = bf16[1,1024,768]{2,1,0:T(8,128)(2,1)} async-done(((bf16[1,256,768]{2,1,0:T(8,128)(2,1)}), bf16[1,1024,768]{2,1,0:T(8,128)(2,1)}) %all-gather.11.cloned.1.call-update) | async-done | bytes 1572880 | tf_op jit(solution)/shard_map/all_gather | solution.py:21
  204.9 4.9 fusion.25
  209.7 19.7 %all-gather.15.cloned.1.call-done = bf16[768,768]{0,1:T(8,128)(2,1)} async-done(((bf16[768,96]{0,1:T(8,128)(2,1)}), bf16[768,768]{0,1:T(8,128)(2,1)}) %all-gather.15.cloned.1.call-update) | async-done | bytes 1179664 | tf_op jit(solution)/shard_map/all_gather | solution.py:165
  229.4 38.5 %all-gather.17.cloned.1.call-done = bf16[1,1024,768]{2,1,0:T(8,128)(2,1)} async-done(((bf16[1,256,768]{2,1,0:T(8,128)(2,1)}), bf16[1,1024,768]{2,1,0:T(8,128)(2,1)}) %all-gather.17.cloned.1.call-update) | async-done | bytes 1572880 | tf_op jit(solution)/shard_map/all_gather | solution.py:21
  268.0 6.9 %convert_reduce_fusion = (f32[768]{0:T(1024)}, bf16[1024,768]{1,0:T(8,128)(2,1)S(1)}) fusion(bf16[768,768]{0,1:T(8,128)(2,1)} %all-gather.15.cloned.1.call-done, bf16[1,1024,768]{2,1,0:T(8,128)(2,1)} %all-gather.17.cloned.1.call-done, f32[1024,768]{1,0:T(8,128)} %fusion.25, f32[768]{0:T(1024)S(1)} %reshape.433), kind=kOutput, calls=%fused_computation.17 | convolution fusion | flops 1229192448 | bytes 7477248 | tf_op jit(solution)/shard_map/rd,fd->rf/dot_general | solution.py:201
  278.7 5.5 fusion.47
  284.9 28.0 %reduce-scatter.20.cloned.1.call-done = bf16[1,256,768]{2,1,0:T(8,128)(2,1)} async-done(((bf16[1,1024,768]{2,1,0:T(8,128)(2,1)}), bf16[1,256,768]{2,1,0:T(8,128)(2,1)}) %reduce-scatter.20.cloned.1.call-update) | async-done | bytes 393232 | tf_op jit(solution)/shard_map/reduce_scatter | solution.py:25
  315.5 33.8 %reduce-scatter.18.cloned.1.call-done = bf16[1,256,768]{2,1,0:T(8,128)(2,1)} async-done(((bf16[1,1024,768]{2,1,0:T(8,128)(2,1)}), bf16[1,256,768]{2,1,0:T(8,128)(2,1)}) %reduce-scatter.18.cloned.1.call-update) | async-done | bytes 393232 | tf_op jit(solution)/shard_map/reduce_scatter | solution.py:25
  354.5 35.7 %all-gather.19.cloned.1.call-done = bf16[1,1024,768]{2,1,0:T(8,128)(2,1)} async-done(((bf16[1,256,768]{2,1,0:T(8,128)(2,1)}), bf16[1,1024,768]{2,1,0:T(8,128)(2,1)}) %all-gather.19.cloned.1.call-update) | async-done | bytes 1572880 | tf_op jit(solution)/shard_map/all_gather | solution.py:21
  401.2 4.1 multiply_reduce_fusion
  405.4 4.4 convert_reduce_fusion.6
  418.9 5.7 fusion.17
  425.0 4.7 fusion.23
  441.3 31.3 %reduce-scatter.22.cloned.1.call-done = bf16[1,256,768]{2,1,0:T(8,128)(2,1)} async-done(((bf16[1,1024,768]{2,1,0:T(8,128)(2,1)}), bf16[1,256,768]{2,1,0:T(8,128)(2,1)}) %reduce-scatter.22.cloned.1.call-update) | async-done | bytes 393232 | tf_op jit(solution)/shard_map/reduce_scatter | solution.py:25
  478.4 24.2 %all-reduce.17 = (f32[768]{0:T(1024)S(1)}, f32[768]{0:T(1024)S(1)}, f32[3,64]{1,0:T(4,128)S(1)}, f32[3,64]{1,0:T(4,128)S(1)}, f32[768]{0:T(1024)S(1)}, /*index=5...) all-reduce(f32[768]{0:T(1024)S(1)} %get-tuple-element.151, ...), channel_id=6, replica_groups=mesh['dp'=8,'mp'=4] {'dp'}, use_global_device_ids=true, to_apply=%region_19.20.clone | all-reduce | flops 5760 | bytes 46080
  503.8 10.2 %all-reduce.18 = (f32[96]{0:T(128)}, f32[96]{0:T(128)}, f32[96]{0:T(128)}, f32[96]{0:T(128)}, f32[96]{0:T(128)}, /*index=5*/f32[96]{0:T(128)}) all-reduce(f32[96]{0:T(128)S(1)} %dynamic-slice.32, f32[96]{0:T(128)S(1)} %dynamic-slice.34, f32[96]{0:T(128)S(1)} %dynamic-slice.40, ...), channel_id=1, replica_groups=mesh['dp'=8,'mp'=4] {'mp'}, use_global_device_ids=true, to_apply=%region_20.21 | all-reduce | flops 576 | bytes 4608 | tf_op jit(solution)/shard_map/psum | solution.py:269
  517.7 46.5 %reduce-scatter.30.cloned.1.call-done = f32[96,768]{1,0:T(8,128)} async-done(((f32[768,768]{1,0:T(8,128)}), f32[96,768]{1,0:T(8,128)}) %reduce-scatter.30.cloned.1.call-update) | async-done | bytes 294928 | tf_op jit(solution)/shard_map/reduce_scatter | solution.py:262
  564.2 38.7 %reduce-scatter.28.cloned.1.call-done = f32[96,192]{1,0:T(8,128)} async-done(((f32[768,192]{1,0:T(8,128)}), f32[96,192]{1,0:T(8,128)}) %reduce-scatter.28.cloned.1.call-update) | async-done | bytes 73744 | tf_op jit(solution)/shard_map/reduce_scatter | solution.py:258
  602.9 38.6 %reduce-scatter.24.cloned.1.call-done = f32[96,192]{1,0:T(8,128)} async-done(((f32[768,192]{1,0:T(8,128)}), f32[96,192]{1,0:T(8,128)}) %reduce-scatter.24.cloned.1.call-update) | async-done | bytes 73744 | tf_op jit(solution)/shard_map/reduce_scatter | solution.py:255
  641.5 38.7 %reduce-scatter.26.cloned.1.call-done = f32[96,192]{1,0:T(8,128)} async-done(((f32[768,192]{1,0:T(8,128)}), f32[96,192]{1,0:T(8,128)}) %reduce-scatter.26.cloned.1.call-update) | async-done | bytes 73744 | tf_op jit(solution)/shard_map/reduce_scatter | solution.py:257
  (248 shorter events, 85.4 us)
Async XLA Ops:
  8.0 74.4 %copy-start.32 = (bf16[96,192]{1,0:T(8,128)(2,1)S(1)}, bf16[96,192]{1,0:T(8,128)(2,1)}, u32[]{:S(2)}) copy-start(bf16[96,192]{1,0:T(8,128)(2,1)} %param.35) | copy-start | bytes 110596
  8.0 83.5 %copy-start.33 = (bf16[96,192]{1,0:T(8,128)(2,1)S(1)}, bf16[96,192]{1,0:T(8,128)(2,1)}, u32[]{:S(2)}) copy-start(bf16[96,192]{1,0:T(8,128)(2,1)} %param.36) | copy-start | bytes 110596
  8.0 95.0 %all-gather.9.cloned.1.call-start = ((), (), s32[]{:S(2)}) async-start(), calls=%async_computation.10 | async-start | bytes 1966080 | tf_op jit(solution)/shard_map/all_gather | solution.py:21
  10.5 94.8 %copy-start.36 = (f32[256]{0:T(256)}, f32[256]{0:T(256)S(1)}, u32[]{:S(2)}) copy-start(f32[256]{0:T(256)S(1)} %fusion.116) | copy-start | bytes 3076
  45.1 119.3 %reduce-scatter.16.cloned.1.call-start = ((), (), s32[]{:S(2)}) async-start(), calls=%async_computation.11 | async-start | bytes 1966080 | tf_op jit(solution)/shard_map/reduce_scatter | solution.py:25
  73.4 53.4 %copy-start.4 = (bf16[192,768]{0,1:T(8,128)(2,1)}, bf16[192,768]{0,1:T(8,128)(2,1)S(1)}, u32[]{:S(2)}) copy-start(bf16[192,768]{0,1:T(8,128)(2,1)S(1)} %all_gather.71) | copy-start | bytes 884740
  126.7 42.1 %copy-start.26 = (bf16[3,64,512]{2,1,0:T(8,128)(2,1)}, bf16[3,64,512]{2,1,0:T(8,128)(2,1)S(1)}, u32[]{:S(2)}) copy-start(bf16[3,64,512]{2,1,0:T(8,128)(2,1)S(1)} %fusion.90) | copy-start | bytes 589828
  128.6 41.7 %copy-start.52 = (bf16[12,8]{0,1:T(8,128)(2,1)S(1)}, bf16[12,8]{0,1:T(8,128)(2,1)}, u32[]{:S(2)}) copy-start(bf16[12,8]{0,1:T(8,128)(2,1)} %param.43) | copy-start | bytes 580
  128.6 50.8 %all-gather.13.cloned.1.call-start = ((), (), s32[]{:S(2)}) async-start(), calls=%async_computation.13 | async-start | bytes 1327104 | tf_op jit(solution)/shard_map/all_gather | solution.py:163
  129.2 75.7 %all-gather.11.cloned.1.call-start = ((), (), s32[]{:S(2)}) async-start(), calls=%async_computation.12 | async-start | bytes 1966080 | tf_op jit(solution)/shard_map/all_gather | solution.py:21
  165.6 147.4 %copy-start.35 = (f32[256]{0:T(256)}, f32[256]{0:T(256)S(1)}, u32[]{:S(2)}) copy-start(f32[256]{0:T(256)S(1)} %broadcast_multiply_fusion) | copy-start | bytes 3076
  166.8 146.1 %copy-start.41 = (f32[256]{0:T(256)}, f32[256]{0:T(256)S(1)}, u32[]{:S(2)}) copy-start(f32[256]{0:T(256)S(1)} %fusion.117) | copy-start | bytes 3076
  168.9 60.6 %all-gather.15.cloned.1.call-start = ((), (), s32[]{:S(2)}) async-start(), calls=%async_computation.14 | async-start | bytes 1327104 | tf_op jit(solution)/shard_map/all_gather | solution.py:165
  169.4 98.5 %all-gather.17.cloned.1.call-start = ((), (), s32[]{:S(2)}) async-start(), calls=%async_computation.16 | async-start | bytes 1966080 | tf_op jit(solution)/shard_map/all_gather | solution.py:21
  170.2 142.8 %reduce-scatter.20.cloned.1.call-start = ((), (), s32[]{:S(2)}) async-start(), calls=%async_computation.17 | async-start | bytes 1966080 | tf_op jit(solution)/shard_map/reduce_scatter | solution.py:25
  179.4 99.3 %copy-start.50 = (f32[768]{0:T(1024)}, f32[768]{0:T(1024)S(1)}, u32[]{:S(2)}) copy-start(f32[768]{0:T(1024)S(1)} %reshape.433) | copy-start | bytes 9220
  278.7 70.7 %reduce-scatter.18.cloned.1.call-start = ((), (), s32[]{:S(2)}) async-start(), calls=%async_computation.15 | async-start | bytes 1966080 | tf_op jit(solution)/shard_map/reduce_scatter | solution.py:25
  284.3 106.0 %all-gather.19.cloned.1.call-start = ((), (), s32[]{:S(2)}) async-start(), calls=%async_computation.18 | async-start | bytes 1966080 | tf_op jit(solution)/shard_map/all_gather | solution.py:21
  351.7 43.7 %copy-start.42 = (f32[256]{0:T(256)}, f32[256]{0:T(256)S(1)}, u32[]{:S(2)}) copy-start(f32[256]{0:T(256)S(1)} %negate_multiply_fusion.1) | copy-start | bytes 3076
  354.3 85.4 %reduce-scatter.34.cloned.1.call-start = ((), (), s32[]{:S(2)}) async-start(), calls=%async_computation.25 | async-start | bytes 884736
  401.1 71.5 %reduce-scatter.22.cloned.1.call-start = ((), (), s32[]{:S(2)}) async-start(), calls=%async_computation.19 | async-start | bytes 1966080 | tf_op jit(solution)/shard_map/reduce_scatter | solution.py:25
  418.9 98.8 %reduce-scatter.32.cloned.1.call-start = ((), (), s32[]{:S(2)}) async-start(), calls=%async_computation.24 | async-start | bytes 2654208 | tf_op jit(solution)/shard_map/reduce_scatter | solution.py:264
  424.7 139.5 %reduce-scatter.30.cloned.1.call-start = ((), (), s32[]{:S(2)}) async-start(), calls=%async_computation.23 | async-start | bytes 2654208 | tf_op jit(solution)/shard_map/reduce_scatter | solution.py:262
  429.8 173.1 %reduce-scatter.28.cloned.1.call-start = ((), (), s32[]{:S(2)}) async-start(), calls=%async_computation.22 | async-start | bytes 884736 | tf_op jit(solution)/shard_map/reduce_scatter | solution.py:258
  432.5 208.9 %reduce-scatter.24.cloned.1.call-start = ((), (), s32[]{:S(2)}) async-start(), calls=%async_computation.20 | async-start | bytes 884736 | tf_op jit(solution)/shard_map/reduce_scatter | solution.py:255
  434.1 40.5 %copy-start.37 = (f32[256]{0:T(256)S(1)}, f32[256]{0:T(256)}, u32[]{:S(2)}) copy-start(f32[256]{0:T(256)} %copy-done.36) | copy-start | bytes 3076
  434.1 42.0 %copy-start.5 = (bf16[1,256,768]{2,1,0:T(8,128)(2,1)S(1)}, bf16[1,256,768]{2,1,0:T(8,128)(2,1)}, u32[]{:S(2)}) copy-start(bf16[1,256,768]{2,1,0:T(8,128)(2,1)} %param.30) | copy-start | bytes 1179652
  434.1 246.1 %reduce-scatter.26.cloned.1.call-start = ((), (), s32[]{:S(2)}) async-start(), calls=%async_computation.21 | async-start | bytes 884736 | tf_op jit(solution)/shard_map/reduce_scatter | solution.py:257
  439.6 38.8 %copy-start.39 = (f32[768]{0:T(1024)S(1)}, f32[768]{0:T(1024)}, u32[]{:S(2)}) copy-start(f32[768]{0:T(1024)} %get-tuple-element.153) | copy-start | bytes 9220
  439.6 38.8 %copy-start.40 = (f32[768]{0:T(1024)S(1)}, f32[768]{0:T(1024)}, u32[]{:S(2)}) copy-start(f32[768]{0:T(1024)} %get-tuple-element.177) | copy-start | bytes 9220
  439.6 38.8 %copy-start.46 = (f32[3,64]{1,0:T(4,128)S(1)}, f32[3,64]{1,0:T(4,128)}, u32[]{:S(2)}) copy-start(f32[3,64]{1,0:T(4,128)} %reshape.429) | copy-start | bytes 2308
  439.6 38.8 %copy-start.54 = (f32[3,64]{1,0:T(4,128)S(1)}, f32[3,64]{1,0:T(4,128)}, u32[]{:S(2)}) copy-start(f32[3,64]{1,0:T(4,128)} %get-tuple-element.198) | copy-start | bytes 2308
  (45 other events, 352.2 us)
Sparse Core Ops, SparseCore 0:
  45.2 36.9 all-gather.8
  128.7 35.5 reduce-scatter.15
  278.8 34.1 reduce-scatter.19
  315.1 34.2 reduce-scatter.17
Sparse Core Ops, SparseCore 1:
  131.0 24.1 all-gather.12
  168.9 35.9 all-gather.10
  206.6 22.7 all-gather.14
  231.0 36.9 all-gather.16
  354.4 35.9 all-gather.18
  401.2 33.8 reduce-scatter.33
  437.3 35.3 reduce-scatter.21
  476.4 41.2 reduce-scatter.31
  521.8 42.3 reduce-scatter.29
  567.9 34.9 reduce-scatter.27
  606.5 34.9 reduce-scatter.23
  645.2 34.9 reduce-scatter.25
where the time goes:
time: 693 us; the launch traced here: 688 us
  waiting for transfers between devices  415 us (60%)
  blocking collectives  123 us (18%)
  matrix products  81.8 us (12%)
  other arithmetic  30.2 us (4%)
  local copies, waits for them, and re-layouts  18.4 us (3%)
  between operations  18.4 us (3%)
    reduce_scatter x4, waiting for transfers between devices, scatter_rows(): lax.psum_scatter(v.astype(jnp.bfloat16), 'mp', scatter_dimension=1, tiled...  128 us
    all_gather x4, waiting for transfers between devices, gather_rows(): return lax.all_gather(v, 'mp', axis=1, tiled=True)  99.8 us
    unnamed x2, blocking collectives  49.7 us
    reduce_scatter x1, waiting for transfers between devices, local(): lax.psum_scatter(grad_expand, 'dp', scatter_dimension=0, tiled=True)  46.5 us
    reduce_scatter x1, waiting for transfers between devices, local(): lax.psum_scatter(grad_key, 'dp', scatter_dimension=0, tiled=True)  38.7 us
    reduce_scatter x1, waiting for transfers between devices, local(): lax.psum_scatter(grad_value, 'dp', scatter_dimension=0, tiled=True)  38.7 us
    reduce_scatter x1, waiting for transfers between devices, local(): lax.psum_scatter(grad_query, 'dp', scatter_dimension=0, tiled=True)  38.6 us
    all_gather x1, waiting for transfers between devices, local(): lax.all_gather(w_reduce, 'dp', axis=1, tiled=True)  19.7 us
  transfers between devices with their start and end apart: 16, of which 13 were waited for; matrix products, arithmetic and copies ran while one was open for 10% of the time, Pallas kernels for 0%

commit v1 on v0

v1 whole, which is shorter than its diff:
```python
import jax
import jax.numpy as jnp
from jax import lax
from jax.sharding import PartitionSpec as P

HD = 64
F32 = jnp.float32
BF16 = jnp.bfloat16


def norm_stats(v):
    mean = jnp.mean(v, axis=-1, keepdims=True)
    centered = v - mean
    spread = jnp.mean(centered * centered, axis=-1, keepdims=True)
    rstd = lax.rsqrt(spread + 1e-05)
    return centered * rstd, rstd


def norm_back(grad, xhat, rstd, gain):
    e = grad * gain
    mean_e = jnp.mean(e, axis=-1, keepdims=True)
    mean_ex = jnp.mean(e * xhat, axis=-1, keepdims=True)
    return rstd * (e - mean_e - xhat * mean_ex)


def gelu_tanh(v):
    return 0.5 * v * (1.0 + jnp.tanh(0.7978845608028654 * (v + 0.044715 * v * v * v)))


def dot(a, b):
    return jnp.dot(a, b, preferred_element_type=F32)


def dot_tn(a, b):
    return lax.dot_general(a, b, (((0,), (0,)), ((), ())), preferred_element_type=F32)


def dot_nt(a, b):
    return lax.dot_general(a, b, (((1,), (1,)), ((), ())), preferred_element_type=F32)


def gather_rows(v):
    return lax.all_gather(v, "mp", axis=0, tiled=True)


def scatter_rows(v):
    return lax.psum_scatter(v.astype(BF16), "mp", scatter_dimension=0, tiled=True).astype(F32)


def block_scores(qhead, khead, first, end, scale):
    scores = (
        jnp.einsum("qhd,khd->hqk", qhead[first:end], khead[:end], preferred_element_type=F32)
        * scale
    )
    causal = (first + jnp.arange(end - first))[:, None] >= jnp.arange(end)[None, :]
    return jnp.where(causal[None], scores, -1e30)


def attend_forward(query, keys, values, heads):
    length = query.shape[0]
    block = min(512, length)
    scale = HD ** (-0.5)
    qhead = query.reshape(length, heads, HD)
    khead = keys.reshape(length, heads, HD)
    vhead = values.reshape(length, heads, HD)
    pieces, maxima, totals = ([], [], [])
    for first in range(0, length, block):
        end = first + block
        scores = block_scores(qhead, khead, first, end, scale)
        top = jnp.max(scores, axis=-1, keepdims=True)
        expo = jnp.exp(scores - top)
        total = jnp.sum(expo, axis=-1, keepdims=True)
        probs = (expo / total).astype(BF16)
        mixed = jnp.einsum("hqk,khd->qhd", probs, vhead[:end], preferred_element_type=F32)
        pieces.append(mixed.reshape(block, heads * HD).astype(BF16))
        maxima.append(top)
        totals.append(total)
    return (jnp.concatenate(pieces, 0), maxima, totals)


def attend_backward(query, keys, values, d_mixed, maxima, totals, heads):
    length = query.shape[0]
    block = min(512, length)
    scale = HD ** (-0.5)
    qhead = query.reshape(length, heads, HD)
    khead = keys.reshape(length, heads, HD)
    vhead = values.reshape(length, heads, HD)
    dhead = d_mixed.reshape(length, heads, HD)
    key_acc = jnp.zeros((length, heads, HD), F32)
    value_acc = jnp.zeros((length, heads, HD), F32)
    query_parts = []
    for number, first in enumerate(range(0, length, block)):
        end = first + block
        scores = block_scores(qhead, khead, first, end, scale)
        probs = jnp.exp(scores - maxima[number]) / totals[number]
        d_probs = jnp.einsum(
            "qhd,khd->hqk", dhead[first:end], vhead[:end], preferred_element_type=F32
        )
        inner = jnp.sum(probs * d_probs, axis=-1, keepdims=True)
        d_scores = (probs * (d_probs - inner)).astype(BF16)
        d_query = (
            jnp.einsum("hqk,khd->qhd", d_scores, khead[:end], preferred_element_type=F32) * scale
        )
        query_parts.append(d_query.reshape(block, heads * HD).astype(BF16))
        key_acc = key_acc.at[:end].add(
            jnp.einsum("hqk,qhd->khd", d_scores, qhead[first:end], preferred_element_type=F32)
            * scale
        )
        value_acc = value_acc.at[:end].add(
            jnp.einsum(
                "hqk,qhd->khd", probs.astype(BF16), dhead[first:end], preferred_element_type=F32
            )
        )
    d_keys = key_acc.reshape(length, heads * HD).astype(BF16)
    d_values = value_acc.reshape(length, heads * HD).astype(BF16)
    return (jnp.concatenate(query_parts, 0), d_keys, d_values)


def local(
    tokens,
    cotangent,
    first_gain,
    first_shift,
    w_query,
    b_query,
    w_key,
    w_value,
    b_value,
    w_out,
    b_out,
    second_gain,
    second_shift,
    w_expand,
    b_expand,
    w_reduce,
    b_reduce,
):
    part, ecols = w_query.shape
    fcols = w_expand.shape[1]
    hrows, hcols = b_query.shape
    frows, _ = b_expand.shape
    bias_len = hrows * hcols
    heads_bias = jnp.concatenate([b_query.reshape(-1), b_value.reshape(-1)])
    heads_bias = jnp.pad(heads_bias, (0, part - 2 * bias_len))
    columns = jnp.stack(
        [
            first_gain,
            first_shift,
            b_out,
            second_gain,
            second_shift,
            b_reduce,
            b_expand.reshape(-1),
            heads_bias,
        ],
        axis=1,
    )
    columns = jnp.pad(columns, ((0, 0), (0, 120)))
    token_rows = gather_rows(tokens[0])
    attn_pack = lax.all_gather(
        jnp.concatenate([w_query, w_key, w_value, w_out.T, columns], axis=1), "dp", tiled=True
    )
    mlp_pack = lax.all_gather(
        jnp.concatenate([w_expand, w_reduce.T], axis=1), "dp", tiled=True
    )
    out_rows = gather_rows(cotangent[0])
    width = attn_pack.shape[0]
    ways = width // part
    w_qkv = attn_pack[:, : 3 * ecols]
    w_out_t = attn_pack[:, 3 * ecols : 4 * ecols]
    vectors = attn_pack[:, 4 * ecols : 4 * ecols + 8].astype(F32).T
    gain_one, shift_one, bias_out = vectors[0:1], vectors[1:2], vectors[2:3]
    gain_two, shift_two, bias_red = vectors[3:4], vectors[4:5], vectors[5:6]
    bias_exp = vectors[6].reshape(ways, frows, hcols).transpose(1, 0, 2).reshape(1, -1)
    bias_heads = vectors[7].reshape(ways, part)
    bias_q = bias_heads[:, :bias_len].reshape(ways, hrows, hcols).transpose(1, 0, 2)
    bias_v = bias_heads[:, bias_len : 2 * bias_len].reshape(ways, hrows, hcols)
    bias_v = bias_v.transpose(1, 0, 2)
    bias_qkv = jnp.concatenate(
        [bias_q.reshape(1, -1), jnp.zeros((1, ecols), F32), bias_v.reshape(1, -1)], axis=1
    )
    w_exp = mlp_pack[:, :fcols]
    w_red_t = mlp_pack[:, fcols:]

    xhat_all, _ = norm_stats(token_rows.astype(F32))
    rows_one = (xhat_all * gain_one + shift_one).astype(BF16)
    qkv = (dot(rows_one, w_qkv) + bias_qkv).astype(BF16)
    query, keys, values = qkv[:, :ecols], qkv[:, ecols : 2 * ecols], qkv[:, 2 * ecols :]
    heads = ecols // HD
    mixed, maxima, totals = attend_forward(query, keys, values, heads)
    partial_one = dot_nt(mixed, w_out_t)
    shard = tokens[0].astype(F32)
    hidden = shard + scatter_rows(partial_one) + bias_out
    xhat_two, rstd_two = norm_stats(hidden)
    rows_two = gather_rows((xhat_two * gain_two + shift_two).astype(BF16))
    pre = dot(rows_two, w_exp) + bias_exp
    act_full, back_gelu = jax.vjp(gelu_tanh, pre)
    act = act_full.astype(BF16)
    (d_pre_full,) = back_gelu(dot(out_rows, w_red_t))
    d_pre = d_pre_full.astype(BF16)
    d_second = scatter_rows(dot_nt(d_pre, w_exp))
    partial_two = dot_nt(act, w_red_t)
    result = (hidden + scatter_rows(partial_two) + bias_red).astype(BF16)
    mlp_grads = jnp.concatenate([dot_tn(rows_two, d_pre), dot_tn(out_rows, act)], axis=1)
    mlp_owned = lax.psum_scatter(
        mlp_grads.astype(BF16), "dp", scatter_dimension=0, tiled=True
    ).astype(F32)
    grad_out = cotangent[0].astype(F32)
    grad_bexpand = jnp.sum(d_pre.astype(F32), axis=0)

    grad_gain_two = jnp.sum(d_second * xhat_two, axis=0)
    grad_shift_two = jnp.sum(d_second, axis=0)
    d_hidden = grad_out + norm_back(d_second, xhat_two, rstd_two, gain_two)
    d_hidden_low = d_hidden.astype(BF16)
    hidden_rows = gather_rows(d_hidden_low)
    grad_bout = jnp.sum(d_hidden_low.astype(F32), axis=0)
    grad_breduce = jnp.sum(grad_out, axis=0)
    d_mixed = dot(hidden_rows, w_out_t).astype(BF16)
    d_query, d_keys, d_values = attend_backward(
        query, keys, values, d_mixed, maxima, totals, heads
    )
    d_qkv = jnp.concatenate([d_query, d_keys, d_values], axis=1)
    d_first = scatter_rows(dot_nt(d_qkv, w_qkv))
    attn_grads = jnp.concatenate([dot_tn(rows_one, d_qkv), dot_tn(hidden_rows, mixed)], axis=1)
    attn_owned = lax.psum_scatter(
        attn_grads.astype(BF16), "dp", scatter_dimension=0, tiled=True
    ).astype(F32)
    grad_bq = jnp.sum(d_query.astype(F32), axis=0)
    grad_bv = jnp.sum(d_values.astype(F32), axis=0)

    xhat_one, rstd_one = norm_stats(shard)
    grad_gain_one = jnp.sum(d_first * xhat_one, axis=0)
    grad_shift_one = jnp.sum(d_first, axis=0)
    grad_tokens = d_hidden + norm_back(d_first, xhat_one, rstd_one, gain_one)
    spread = lax.psum(
        jnp.stack(
            [grad_gain_one, grad_shift_one, grad_bout, grad_gain_two, grad_shift_two, grad_breduce]
        ),
        ("dp", "mp"),
    )
    ranks = lax.psum(jnp.concatenate([grad_bq, grad_bv, grad_bexpand]), "dp")
    me = lax.axis_index("dp")
    spread = lax.dynamic_slice_in_dim(spread, me * part, part, 1)
    ranks = lax.dynamic_slice_in_dim(ranks.reshape(-1, HD), me * hcols, hcols, 1)
    return (
        result[None],
        grad_tokens[None],
        spread[0],
        spread[1],
        attn_owned[:, :ecols],
        ranks[:hrows],
        attn_owned[:, ecols : 2 * ecols],
        attn_owned[:, 2 * ecols : 3 * ecols],
        ranks[hrows : 2 * hrows],
        attn_owned[:, 3 * ecols :].T,
        spread[2],
        spread[3],
        spread[4],
        mlp_owned[:, :fcols],
        ranks[2 * hrows :],
        mlp_owned[:, fcols:].T,
        spread[5],
    )


def solution(mesh):
    rows, vec = P("dp", "mp", None), P("dp")
    down, across = P("dp", "mp"), P("mp", "dp")
    params = (
        vec, vec, down, across, down, down, across, across, vec, vec, vec, down, across, across,
        vec,
    )
    return jax.shard_map(
        local,
        mesh=mesh,
        in_specs=(rows, rows) + params,
        out_specs=(rows, rows) + params,
        check_vma=False,
    )
```

time: 693 us -> 547 us (0.79)
  waiting for transfers between devices: 415 us -> 348 us
  blocking collectives: 123 us -> 62.6 us
  matrix products: 81.8 us -> 61.7 us
    reduce_scatter x9 -> x4, waiting for transfers between devices: 294 us -> 131 us  [scatter_rows(): lax.psum_scatter(v.astype(BF16), 'mp', scatter_dimension=0, tiled=True)]
    all_gather x7 -> x0, blocking collectives: 62.7 us -> none  [the longest x1 9.55 us: local(): lax.all_gather(w_value, 'dp', axis=0, tiled=True)]
    all_gather x6, waiting for transfers between devices: 119 us -> 181 us  [the longest x4 133 us: gather_rows(): return lax.all_gather(v, 'mp', axis=0, tiled=True)]
    psum x1 -> x2, blocking collectives: 10.2 us -> 62.6 us  [the longest x1 39.4 us: local(): lax.psum(jnp.stack([grad_gain_one, grad_shift_one, grad_bout, grad_gain_t...]
    unnamed x2 -> x0, blocking collectives: 49.7 us -> none
    unnamed x17 -> x14, waiting for transfers between devices: 1.97 us -> 36.4 us
    dot_general x21 -> x16, matrix products: 60.3 us -> 45.2 us  [the longest x4 15.6 us: dot(): return jnp.dot(a, b, preferred_element_type=F32)]
    reduce_sum x11 -> x10, other arithmetic: 18 us -> 13.7 us  [the longest x2 3.39 us: norm_stats(): spread = jnp.mean(centered * centered, axis=-1, keepdims=True)]
  transfers between devices with their start and end apart: 16 -> 12, of which waited for: 13 -> 12; matrix products, arithmetic and copies ran while one was open for 10% -> 12% of each run, Pallas kernels for 0% -> 0%
where the time goes in v1:
time: 547 us; the launch traced here: 538 us
  waiting for transfers between devices  348 us (64%)
  blocking collectives  62.6 us (11%)
  matrix products  61.7 us (11%)
  local copies, waits for them, and re-layouts  25.1 us (5%)
  other arithmetic  23.9 us (4%)
  between operations  15.5 us (3%)
    all_gather x4, waiting for transfers between devices, gather_rows(): return lax.all_gather(v, 'mp', axis=0, tiled=True)  133 us
    reduce_scatter x4, waiting for transfers between devices, scatter_rows(): lax.psum_scatter(v.astype(BF16), 'mp', scatter_dimension=0, tiled=True)  131 us
    psum x1, blocking collectives, local(): lax.psum(jnp.stack([grad_gain_one, grad_shift_one, grad_bout, grad_gain_t...  39.4 us
    unnamed x14, waiting for transfers between devices  36.4 us
    all_gather x1, waiting for transfers between devices, local(): lax.all_gather(jnp.concatenate([w_expand, w_reduce.T], axis=1), 'dp', til...  24.8 us
    psum x1, blocking collectives, local(): ranks = lax.psum(jnp.concatenate([grad_bq, grad_bv, grad_bexpand]), 'dp')  23.2 us
    all_gather x1, waiting for transfers between devices, local(): lax.all_gather(jnp.concatenate([w_query, w_key, w_value, w_out.T, columns...  22.4 us
    dot_general x4, matrix products, dot(): return jnp.dot(a, b, preferred_element_type=F32)  15.6 us
  transfers between devices with their start and end apart: 12, of which 12 were waited for; matrix products, arithmetic and copies ran while one was open for 12% of the time, Pallas kernels for 0%

profile of v1, /device:TPU:0, one launch (start us, length us, event | category | flops | bytes accessed | tf_op | source)
XLA Modules:
  0.0 537.8 jit_solution(3074433430725644306)
XLA Ops:
  16.0 33.4 %all-gather.17.cloned.1.call-done = bf16[1,1024,768]{2,1,0:T(8,128)(2,1)} async-done(((bf16[1,256,768]{2,1,0:T(8,128)(2,1)}), bf16[1,1024,768]{2,1,0:T(8,128)(2,1)}) %all-gather.17.cloned.1.call-update) | async-done | bytes 1572880 | tf_op jit(solution)/shard_map/all_gather | solution.py:43
  51.1 2.1 fusion.6
  53.3 22.4 %all-gather.9.cloned.1.call-done = bf16[768,896]{1,0:T(8,128)(2,1)} async-done(((bf16[96,896]{1,0:T(8,128)(2,1)}), bf16[768,896]{1,0:T(8,128)(2,1)}) %all-gather.9.cloned.1.call-update) | async-done | bytes 1376272 | tf_op jit(solution)/shard_map/all_gather | solution.py:160
  82.0 3.2 fusion.120
  85.2 2.2 convolution_convert_fusion.8
  87.4 6.1 %fusion.119 = (f32[3,512]{1,0:T(4,128)S(1)}, f32[3,512,1024]{2,1,0:T(8,128)}) fusion(pred[512,1024]{1,0:T(8,128)(4,1)} %iota_compare_fusion, bf16[512,3,64]{0,2,1:T(8,128)(2,1)} %bitcast.205, bf16[1024,3,64]{0,2,1:T(8,128)(2,1)S(1)} %bitcast.203), kind=kOutput, calls=%fused_computation.194 | convolution fusion | flops 207619072 | bytes 7411712 | tf_op jit(solution)/shard_map/sub | solution.py:71
  94.2 4.0 fusion.54
  98.8 3.0 convolution_convert_fusion.3
  102.8 34.6 %reduce-scatter.11.cloned.1.call-done = bf16[256,768]{1,0:T(8,128)(2,1)} async-done(((bf16[1024,768]{1,0:T(8,128)(2,1)}), bf16[256,768]{1,0:T(8,128)(2,1)}) %reduce-scatter.11.cloned.1.call-update) | async-done | bytes 393232 | tf_op jit(solution)/shard_map/reduce_scatter | solution.py:47
  142.8 24.8 %all-gather.13.cloned.1.call-done = bf16[768,1536]{1,0:T(8,128)(2,1)} async-done(((bf16[96,1536]{1,0:T(8,128)(2,1)}), bf16[768,1536]{1,0:T(8,128)(2,1)}) %all-gather.13.cloned.1.call-update) | async-done | bytes 2359312 | tf_op jit(solution)/shard_map/all_gather | solution.py:163
  167.7 39.1 %all-gather.11.cloned.1.call-done = bf16[1024,768]{1,0:T(8,128)(2,1)} async-done(((bf16[256,768]{1,0:T(8,128)(2,1)}), bf16[1024,768]{1,0:T(8,128)(2,1)}) %all-gather.11.cloned.1.call-update) | async-done | bytes 1572880 | tf_op jit(solution)/shard_map/all_gather | solution.py:43
  206.8 4.8 fusion.66
  211.6 32.7 %all-gather.19.cloned.1.call-done = bf16[1,1024,768]{2,1,0:T(8,128)(2,1)} async-done(((bf16[1,256,768]{2,1,0:T(8,128)(2,1)}), bf16[1,1024,768]{2,1,0:T(8,128)(2,1)}) %all-gather.19.cloned.1.call-update) | async-done | bytes 1572880 | tf_op jit(solution)/shard_map/all_gather | solution.py:43
  244.2 7.0 %convert_reduce_fusion.1 = (f32[768]{0:T(1024)}, bf16[1024,768]{1,0:T(8,128)(2,1)S(1)}) fusion(bf16[768,1536]{1,0:T(8,128)(2,1)} %all-gather.13.cloned.1.call-done, bf16[1,1024,768]{2,1,0:T(8,128)(2,1)} %all-gather.19.cloned.1.call-done, f32[1024,768]{1,0:T(8,128)} %fusion.66, f32[768]{0:T(1024)S(1)} %add.191), kind=kOutput, calls=%fused_computation.31 | convolution fusion | flops 1229192448 | bytes 7477248 | tf_op jit(solution)/shard_map/dot_general | solution.py:31
  251.2 2.6 convolution_convert_fusion.1
  253.9 5.5 %convolution_convert_fusion.2 = bf16[1024,768]{1,0:T(8,128)(2,1)} fusion(bf16[768,1536]{1,0:T(8,128)(2,1)} %all-gather.13.cloned.1.call-done, f32[1024,768]{1,0:T(8,128)} %fusion.66, f32[768]{0:T(1024)S(1)} %add.191), kind=kOutput, calls=%fused_computation.47 | convolution fusion | flops 1216610304 | bytes 5901312 | tf_op jit(solution)/shard_map/dot_general | solution.py:39
  259.7 28.5 %reduce-scatter.15.cloned.1.call-done = bf16[256,768]{1,0:T(8,128)(2,1)} async-done(((bf16[1024,768]{1,0:T(8,128)(2,1)}), bf16[256,768]{1,0:T(8,128)(2,1)}) %reduce-scatter.15.cloned.1.call-update) | async-done | bytes 393232 | tf_op jit(solution)/shard_map/reduce_scatter | solution.py:47
  288.1 2.3 fusion.86
  290.4 34.3 %reduce-scatter.13.cloned.1.call-done = bf16[256,768]{1,0:T(8,128)(2,1)} async-done(((bf16[1024,768]{1,0:T(8,128)(2,1)}), bf16[256,768]{1,0:T(8,128)(2,1)}) %reduce-scatter.13.cloned.1.call-update) | async-done | bytes 393232 | tf_op jit(solution)/shard_map/reduce_scatter | solution.py:47
  324.7 3.4 convert_reduce_fusion.8
  328.4 3.0 convolution_convert_fusion.4
  333.5 2.5 copy.109
  336.1 28.2 %all-gather.15.cloned.1.call-done = bf16[1024,768]{1,0:T(8,128)(2,1)} async-done(((bf16[256,768]{1,0:T(8,128)(2,1)}), bf16[1024,768]{1,0:T(8,128)(2,1)}) %all-gather.15.cloned.1.call-update) | async-done | bytes 1572880 | tf_op jit(solution)/shard_map/all_gather | solution.py:43
  364.3 2.5 convolution_convert_fusion.6
  366.9 2.7 multiply_reduce_fusion.1
  382.3 3.8 convolution_convert_fusion
  386.3 22.6 %reduce-scatter.21.cloned.1.call-done = bf16[96,1536]{1,0:T(8,128)(2,1)} async-done(((bf16[768,1536]{1,0:T(8,128)(2,1)}), bf16[96,1536]{1,0:T(8,128)(2,1)}) %reduce-scatter.21.cloned.1.call-update) | async-done | bytes 294928
  412.4 23.2 %psum.15 = f32[18,64]{1,0:T(8,128)S(1)} all-reduce(f32[18,64]{1,0:T(8,128)S(1)} %reshape.312), channel_id=1, replica_groups=mesh['dp'=8,'mp'=4] {'dp'}, use_global_device_ids=true, to_apply=%region_31.32 | all-reduce | flops 1152 | bytes 9216 | tf_op jit(solution)/shard_map/psum | solution.py:241
  436.9 12.4 %reduce-scatter.19.cloned.1.call-done = bf16[96,768]{1,0:T(8,128)(2,1)} async-done(((bf16[768,768]{1,0:T(8,128)(2,1)}), bf16[96,768]{1,0:T(8,128)(2,1)}) %reduce-scatter.19.cloned.1.call-update) | async-done | bytes 147472
  453.3 33.5 %reduce-scatter.17.cloned.1.call-done = bf16[256,768]{1,0:T(8,128)(2,1)} async-done(((bf16[1024,768]{1,0:T(8,128)(2,1)}), bf16[256,768]{1,0:T(8,128)(2,1)}) %reduce-scatter.17.cloned.1.call-update) | async-done | bytes 393232 | tf_op jit(solution)/shard_map/reduce_scatter | solution.py:47
  488.3 39.4 %psum.14 = f32[6,768]{1,0:T(8,128)S(1)} all-reduce(f32[6,768]{1,0:T(8,128)S(1)} %stack.59), channel_id=1, replica_groups=mesh['dp'=8,'mp'=4] {'dp','mp'}, use_global_device_ids=true, to_apply=%region_26.27 | all-reduce | flops 4608 | bytes 36864 | tf_op jit(solution)/shard_map/psum | solution.py:235
  528.4 2.2 fusion.78
  (211 shorter events, 50.5 us)
Async XLA Ops:
  7.2 42.2 %all-gather.17.cloned.1.call-start = ((), (), s32[]{:S(2)}) async-start(), calls=%async_computation.14 | async-start | bytes 1966080 | tf_op jit(solution)/shard_map/all_gather | solution.py:43
  7.9 67.7 %all-gather.9.cloned.1.call-start = ((), (), s32[]{:S(2)}) async-start(), calls=%async_computation.6 | async-start | bytes 1548288 | tf_op jit(solution)/shard_map/all_gather | solution.py:160
  13.9 123.4 %reduce-scatter.11.cloned.1.call-start = ((), (), s32[]{:S(2)}) async-start(), calls=%async_computation.7 | async-start | bytes 1966080 | tf_op jit(solution)/shard_map/reduce_scatter | solution.py:47
  51.1 27.8 %copy-start.2 = (bf16[1,1024,768]{2,1,0:T(8,128)(2,1)S(1)}, bf16[1,1024,768]{2,1,0:T(8,128)(2,1)}, u32[]{:S(2)}) copy-start(bf16[1,1024,768]{2,1,0:T(8,128)(2,1)} %all-gather.17.cloned.1.call-done) | copy-start | bytes 4718596
  51.1 29.2 %copy-start.26 = (f32[1024]{0:T(1024)}, f32[1024]{0:T(1024)S(1)}, u32[]{:S(2)}) copy-start(f32[1024]{0:T(1024)S(1)} %broadcast_multiply_fusion) | copy-start | bytes 12292
  53.3 27.1 %copy-start.37 = (f32[1024]{0:T(1024)}, f32[1024]{0:T(1024)S(1)}, u32[]{:S(2)}) copy-start(f32[1024]{0:T(1024)S(1)} %add_rsqrt_fusion) | copy-start | bytes 12292
  82.0 5.4 copy-start.9
  87.4 6.8 %copy-start.15 = (bf16[1024,192]{0,1:T(8,128)(2,1)S(1)}, bf16[1024,192]{0,1:T(8,128)(2,1)}, u32[]{:S(2)}) copy-start(bf16[1024,192]{0,1:T(8,128)(2,1)} %get-tuple-element.174) | copy-start | bytes 1179652
  94.2 4.7 copy-start.16
  98.2 39.2 %copy-start = (bf16[1,256,768]{2,1,0:T(8,128)(2,1)S(1)}, bf16[1,256,768]{2,1,0:T(8,128)(2,1)}, u32[]{:S(2)}) copy-start(bf16[1,256,768]{2,1,0:T(8,128)(2,1)} %param.29) | copy-start | bytes 1179652
  101.9 40.8 %copy-start.23 = (f32[768]{0:T(1024)S(1)}, f32[768]{0:T(1024)}, u32[]{:S(2)}) copy-start(f32[768]{0:T(1024)} %get-tuple-element.159) | copy-start | bytes 9220
  101.9 65.8 %all-gather.13.cloned.1.call-start = ((), (), s32[]{:S(2)}) async-start(), calls=%async_computation.9 | async-start | bytes 2654208 | tf_op jit(solution)/shard_map/all_gather | solution.py:163
  102.7 104.1 %all-gather.11.cloned.1.call-start = ((), (), s32[]{:S(2)}) async-start(), calls=%async_computation.8 | async-start | bytes 1966080 | tf_op jit(solution)/shard_map/all_gather | solution.py:43
  141.8 102.4 %all-gather.19.cloned.1.call-start = ((), (), s32[]{:S(2)}) async-start(), calls=%async_computation.15 | async-start | bytes 1966080 | tf_op jit(solution)/shard_map/all_gather | solution.py:43
  142.4 145.7 %reduce-scatter.15.cloned.1.call-start = ((), (), s32[]{:S(2)}) async-start(), calls=%async_computation.11 | async-start | bytes 1966080 | tf_op jit(solution)/shard_map/reduce_scatter | solution.py:47
  244.2 7.0 %copy-start.39 = (bf16[768,1536]{1,0:T(8,128)(2,1)S(1)}, bf16[768,1536]{1,0:T(8,128)(2,1)}, u32[]{:S(2)}) copy-start(bf16[768,1536]{1,0:T(8,128)(2,1)} %all-gather.13.cloned.1.call-done) | copy-start | bytes 7077892
  253.8 34.3 %copy-start.1 = (bf16[256,768]{1,0:T(8,128)(2,1)S(1)}, bf16[256,768]{1,0:T(8,128)(2,1)}, u32[]{:S(2)}) copy-start(bf16[256,768]{1,0:T(8,128)(2,1)} %reduce-scatter.11.cloned.1.call-done) | copy-start | bytes 1179652
  253.9 70.9 %reduce-scatter.13.cloned.1.call-start = ((), (), s32[]{:S(2)}) async-start(), calls=%async_computation.10 | async-start | bytes 1966080 | tf_op jit(solution)/shard_map/reduce_scatter | solution.py:47
  259.4 65.3 %copy-start.4 = (bf16[1,256,768]{2,1,0:T(8,128)(2,1)S(1)}, bf16[1,256,768]{2,1,0:T(8,128)(2,1)}, u32[]{:S(2)}) copy-start(bf16[1,256,768]{2,1,0:T(8,128)(2,1)} %param.30) | copy-start | bytes 1179652
  259.4 65.3 %copy-start.28 = (f32[768]{0:T(1024)S(1)}, f32[768]{0:T(1024)}, u32[]{:S(2)}) copy-start(f32[768]{0:T(1024)} %get-tuple-element.158) | copy-start | bytes 9220
  259.5 68.9 %copy-start.40 = (bf16[1024,768]{1,0:T(8,128)(2,1)S(1)}, bf16[1024,768]{1,0:T(8,128)(2,1)}, u32[]{:S(2)}) copy-start(bf16[1024,768]{1,0:T(8,128)(2,1)} %all-gather.11.cloned.1.call-done) | copy-start | bytes 4718596
  259.5 104.9 %all-gather.15.cloned.1.call-start = ((), (), s32[]{:S(2)}) async-start(), calls=%async_computation.12 | async-start | bytes 1966080 | tf_op jit(solution)/shard_map/all_gather | solution.py:43
  328.1 80.8 %reduce-scatter.21.cloned.1.call-start = ((), (), s32[]{:S(2)}) async-start(), calls=%async_computation.17 | async-start | bytes 2654208
  336.0 30.8 %copy-start.18 = (bf16[512,192]{0,1:T(8,128)(2,1)S(1)}, bf16[512,192]{0,1:T(8,128)(2,1)}, u32[]{:S(2)}) copy-start(bf16[512,192]{0,1:T(8,128)(2,1)} %get-tuple-element.172) | copy-start | bytes 589828
  336.0 30.8 %copy-start.32 = (f32[3,512]{1,0:T(4,128)S(1)}, f32[3,512]{1,0:T(4,128)}, u32[]{:S(2)}) copy-start(f32[3,512]{1,0:T(4,128)} %get-tuple-element.193) | copy-start | bytes 18436
  336.0 113.3 %reduce-scatter.19.cloned.1.call-start = ((), (), s32[]{:S(2)}) async-start(), calls=%async_computation.16 | async-start | bytes 1327104
  364.3 7.3 %slice-start = ((s8[6291456]{0:T(1024)(128)(4,1)}), s8[4194304]{0:T(1024)(128)(4,1)S(1)}, s32[]{:S(2)}) async-start(s8[6291456]{0:T(1024)(128)(4,1)} %bitcast.201), calls=%async_computation.18 | async-start | bytes 8388608
  366.9 4.8 slice-start.1
  381.9 4.3 copy-start.35
  382.0 104.8 %reduce-scatter.17.cloned.1.call-start = ((), (), s32[]{:S(2)}) async-start(), calls=%async_computation.13 | async-start | bytes 1966080 | tf_op jit(solution)/shard_map/reduce_scatter | solution.py:47
  386.1 26.1 %copy-start.36 = (f32[768]{0:T(1024)S(1)}, f32[768]{0:T(1024)}, u32[]{:S(2)}) copy-start(f32[768]{0:T(1024)} %get-tuple-element.201) | copy-start | bytes 9220
  410.2 118.2 %copy-start.7 = (f32[256,768]{1,0:T(8,128)S(1)}, f32[256,768]{1,0:T(8,128)}, u32[]{:S(2)}) copy-start(f32[256,768]{1,0:T(8,128)} %get-tuple-element.168) | copy-start | bytes 2359300
  (26 other events, 57.7 us)
Sparse Core Ops, SparseCore 0:
  9.6 39.7 all-gather.16
  51.9 23.7 all-gather.8
  102.0 35.2 reduce-scatter.10
  139.7 27.9 all-gather.12
  169.7 37.0 all-gather.10
  208.2 35.9 all-gather.18
  254.0 34.1 reduce-scatter.14
  290.4 34.2 reduce-scatter.12
  328.2 36.0 all-gather.14
  367.5 41.3 reduce-scatter.20
  412.5 36.7 reduce-scatter.18
  451.5 35.2 reduce-scatter.16

commit v2 on v1

--- a/solution.py
+++ b/solution.py
@@ -1,6 +1,10 @@
+import functools
+
 import jax
 import jax.numpy as jnp
 from jax import lax
+from jax.experimental import pallas as pl
+from jax.experimental.pallas import tpu as pltpu
 from jax.sharding import PartitionSpec as P
 
 HD = 64
@@ -37,6 +41,156 @@
 
 def dot_nt(a, b):
     return lax.dot_general(a, b, (((1,), (1,)), ((), ())), preferred_element_type=F32)
+
+
+def greet(groups):
+    barrier = pltpu.get_barrier_semaphore()
+    for axis, n in groups:
+        me = lax.axis_index(axis)
+        for k in range(1, n):
+            pl.semaphore_signal(
+                barrier,
+                inc=1,
+                device_id={axis: lax.rem(me + k, n)},
+                device_id_type=pl.DeviceIdType.MESH,
+            )
+    pl.semaphore_wait(barrier, sum(n - 1 for _, n in groups))
+
+
+def push(axis, n, k, src, dst, sends, recvs, base=0):
+    copy = pltpu.make_async_remote_copy(
+        src_ref=src,
+        dst_ref=dst,
+        send_sem=sends.at[base + k - 1],
+        recv_sem=recvs.at[base + k - 1],
+        device_id={axis: lax.rem(lax.axis_index(axis) + k, n)},
+        device_id_type=pl.DeviceIdType.MESH,
+    )
+    copy.start()
+    return copy
+
+
+def send_whole(axis, n, src, slots, sends, recvs, base=0):
+    return [push(axis, n, k, src, slots.at[k - 1], sends, recvs, base) for k in range(1, n)]
+
+
+def send_parts(axis, n, parts, slots, sends, recvs, base=0):
+    me = lax.axis_index(axis)
+    return [
+        push(axis, n, k, parts.at[lax.rem(me + k, n)], slots.at[k - 1], sends, recvs, base)
+        for k in range(1, n)
+    ]
+
+
+def send_own(axis, n, src, whole, sends, recvs, base=0):
+    me = lax.axis_index(axis)
+    return [push(axis, n, k, src, whole.at[me], sends, recvs, base) for k in range(1, n)]
+
+
+def settle(copies):
+    for copy in copies:
+        copy.wait()
+
+
+def total_of(axis, parts, slots):
+    total = parts[lax.axis_index(axis)].astype(F32)
+    for k in range(slots.shape[0]):
+        total = total + slots[k].astype(F32)
+    return total
+
+
+def start_kernel(nz, nd, tok, pack, tok_all, pack_all, zs, zr, ds, dr):
+    greet((("mp", nz), ("dp", nd)))
+    copies = send_own("mp", nz, tok, tok_all, zs, zr)
+    copies += send_own("dp", nd, pack, pack_all, ds, dr)
+    tok_all[lax.axis_index("mp")] = tok[...]
+    pack_all[lax.axis_index("dp")] = pack[...]
+    settle(copies)
+
+
+def middle_kernel(nz, part, tok, bias, gain, shift, rows, hidden, slots, own, zs, zr):
+    greet((("mp", nz),))
+    settle(send_parts("mp", nz, part, slots, zs, zr))
+    hid = tok[...].astype(F32) + total_of("mp", part, slots) + bias[...]
+    hidden[...] = hid
+    xhat, _ = norm_stats(hid)
+    own[...] = (xhat * gain[...] + shift[...]).astype(BF16)
+    copies = send_own("mp", nz, own, rows, zs, zr, nz - 1)
+    rows[lax.axis_index("mp")] = own[...]
+    settle(copies)
+
+
+def turn_kernel(nz, part, hidden, cot, gain, rows, d_hidden, vec, slots, own, zs, zr):
+    greet((("mp", nz),))
+    copies = send_parts("mp", nz, part, slots, zs, zr)
+    xhat, rstd = norm_stats(hidden[...])
+    grad_out = cot[...].astype(F32)
+    settle(copies)
+    d_second = total_of("mp", part, slots)
+    d_hid = grad_out + norm_back(d_second, xhat, rstd, gain[...])
+    own[...] = d_hid.astype(BF16)
+    copies = send_own("mp", nz, own, rows, zs, zr, nz - 1)
+    d_hidden[...] = d_hid
+    rows[lax.axis_index("mp")] = own[...]
+    vec[0:1] = jnp.sum(own[...].astype(F32), axis=0, keepdims=True)
+    vec[1:2] = jnp.sum(d_second * xhat, axis=0, keepdims=True)
+    vec[2:3] = jnp.sum(d_second, axis=0, keepdims=True)
+    vec[3:4] = jnp.sum(grad_out, axis=0, keepdims=True)
+    settle(copies)
+
+
+def end_kernel(
+    nz, nd, part, grads, tok, gain, d_hidden, vec, ranks,
+    grad_tok, owned, sums,
+    slots, gslots, mine, zslots, col, dslots, zs, zr, ds, dr,
+):
+    greet((("mp", nz), ("dp", nd)))
+    copies = send_parts("mp", nz, part, slots, zs, zr)
+    others = send_parts("dp", nd, grads, gslots, ds, dr)
+    xhat, rstd = norm_stats(tok[...].astype(F32))
+    settle(copies)
+    d_first = total_of("mp", part, slots)
+    mine[0:1] = jnp.sum(d_first * xhat, axis=0, keepdims=True)
+    mine[1:2] = jnp.sum(d_first, axis=0, keepdims=True)
+    mine[2:6] = vec[0:4]
+    mine[6:8] = jnp.zeros_like(ranks)
+    copies = send_whole("mp", nz, mine, zslots, zs, zr, nz - 1)
+    grad_tok[...] = d_hidden[...] + norm_back(d_first, xhat, rstd, gain[...])
+    settle(copies)
+    total = mine[...]
+    for k in range(nz - 1):
+        total = total + zslots[k]
+    col[0:6] = total[0:6]
+    col[6:8] = ranks[...]
+    copies = send_whole("dp", nd, col, dslots, ds, dr, nd - 1)
+    settle(others)
+    owned[...] = total_of("dp", grads, gslots)
+    settle(copies)
+    total = col[...]
+    for k in range(nd - 1):
+        total = total + dslots[k]
+    sums[...] = total
+
+
+def exchange(kernel, number, outs, scratch, *args):
+    space = pl.BlockSpec(memory_space=pltpu.VMEM)
+    return pl.pallas_call(
+        kernel,
+        out_shape=[jax.ShapeDtypeStruct(*out) for out in outs],
+        in_specs=[space] * len(args),
+        out_specs=[space] * len(outs),
+        scratch_shapes=scratch,
+        compiler_params=pltpu.CompilerParams(
+            collective_id=number, has_side_effects=True, vmem_limit_bytes=40 * 2**20
+        ),
+        cost_estimate=pl.CostEstimate(
+            flops=25_000_000_000, bytes_accessed=60_000_000, transcendentals=0
+        ),
+    )(*args)
+
+
+def sems(count):
+    return [pltpu.SemaphoreType.DMA((count,))] * 2
 
 
 def gather_rows(v):
@@ -156,15 +310,23 @@
         axis=1,
     )
     columns = jnp.pad(columns, ((0, 0), (0, 120)))
-    token_rows = gather_rows(tokens[0])
-    attn_pack = lax.all_gather(
-        jnp.concatenate([w_query, w_key, w_value, w_out.T, columns], axis=1), "dp", tiled=True
-    )
+    nz, nd = lax.axis_size("mp"), lax.axis_size("dp")
+    block, width = tokens.shape[1:]
+    attn_own = jnp.concatenate([w_query, w_key, w_value, w_out.T, columns], axis=1)
+    token_rows, attn_pack = exchange(
+        functools.partial(start_kernel, nz, nd),
+        0,
+        [((nz, block, width), BF16), ((nd,) + attn_own.shape, BF16)],
+        sems(nz - 1) + sems(nd - 1),
+        tokens[0],
+        attn_own,
+    )
+    token_rows = token_rows.reshape(nz * block, width)
+    attn_pack = attn_pack.reshape(width, -1)
     mlp_pack = lax.all_gather(
         jnp.concatenate([w_expand, w_reduce.T], axis=1), "dp", tiled=True
     )
     out_rows = gather_rows(cotangent[0])
-    width = attn_pack.shape[0]
     ways = width // part
     w_qkv = attn_pack[:, : 3 * ecols]
     w_out_t = attn_pack[:, 3 * ecols : 4 * ecols]
@@ -189,56 +351,83 @@
     heads = ecols // HD
     mixed, maxima, totals = attend_forward(query, keys, values, heads)
     partial_one = dot_nt(mixed, w_out_t)
-    shard = tokens[0].astype(F32)
-    hidden = shard + scatter_rows(partial_one) + bias_out
-    xhat_two, rstd_two = norm_stats(hidden)
-    rows_two = gather_rows((xhat_two * gain_two + shift_two).astype(BF16))
+    rows_shape, own_shape = (nz, block, width), (block, width)
+    landing = [pltpu.VMEM((nz - 1, block, width), BF16), pltpu.VMEM(own_shape, BF16)]
+    rows_two, hidden = exchange(
+        functools.partial(middle_kernel, nz),
+        1,
+        [(rows_shape, BF16), (own_shape, F32)],
+        landing + sems(2 * nz - 2),
+        partial_one.astype(BF16).reshape(rows_shape),
+        tokens[0],
+        bias_out,
+        gain_two,
+        shift_two,
+    )
+    rows_two = rows_two.reshape(nz * block, width)
     pre = dot(rows_two, w_exp) + bias_exp
     act_full, back_gelu = jax.vjp(gelu_tanh, pre)
     act = act_full.astype(BF16)
     (d_pre_full,) = back_gelu(dot(out_rows, w_red_t))
     d_pre = d_pre_full.astype(BF16)
-    d_second = scatter_rows(dot_nt(d_pre, w_exp))
+    d_second_part = dot_nt(d_pre, w_exp).astype(BF16).reshape(rows_shape)
+    hidden_rows, d_hidden, vec = exchange(
+        functools.partial(turn_kernel, nz),
+        2,
+        [(rows_shape, BF16), (own_shape, F32), ((4, width), F32)],
+        landing + sems(2 * nz - 2),
+        d_second_part,
+        hidden,
+        cotangent[0],
+        gain_two,
+    )
+    hidden_rows = hidden_rows.reshape(nz * block, width)
     partial_two = dot_nt(act, w_red_t)
     result = (hidden + scatter_rows(partial_two) + bias_red).astype(BF16)
     mlp_grads = jnp.concatenate([dot_tn(rows_two, d_pre), dot_tn(out_rows, act)], axis=1)
     mlp_owned = lax.psum_scatter(
         mlp_grads.astype(BF16), "dp", scatter_dimension=0, tiled=True
     ).astype(F32)
-    grad_out = cotangent[0].astype(F32)
     grad_bexpand = jnp.sum(d_pre.astype(F32), axis=0)
 
-    grad_gain_two = jnp.sum(d_second * xhat_two, axis=0)
-    grad_shift_two = jnp.sum(d_second, axis=0)
-    d_hidden = grad_out + norm_back(d_second, xhat_two, rstd_two, gain_two)
-    d_hidden_low = d_hidden.astype(BF16)
-    hidden_rows = gather_rows(d_hidden_low)
-    grad_bout = jnp.sum(d_hidden_low.astype(F32), axis=0)
-    grad_breduce = jnp.sum(grad_out, axis=0)
     d_mixed = dot(hidden_rows, w_out_t).astype(BF16)
     d_query, d_keys, d_values = attend_backward(
         query, keys, values, d_mixed, maxima, totals, heads
     )
     d_qkv = jnp.concatenate([d_query, d_keys, d_values], axis=1)
-    d_first = scatter_rows(dot_nt(d_qkv, w_qkv))
+    d_first_part = dot_nt(d_qkv, w_qkv).astype(BF16).reshape(rows_shape)
     attn_grads = jnp.concatenate([dot_tn(rows_one, d_qkv), dot_tn(hidden_rows, mixed)], axis=1)
-    attn_owned = lax.psum_scatter(
-        attn_grads.astype(BF16), "dp", scatter_dimension=0, tiled=True
-    ).astype(F32)
     grad_bq = jnp.sum(d_query.astype(F32), axis=0)
     grad_bv = jnp.sum(d_values.astype(F32), axis=0)
 
-    xhat_one, rstd_one = norm_stats(shard)
-    grad_gain_one = jnp.sum(d_first * xhat_one, axis=0)
-    grad_shift_one = jnp.sum(d_first, axis=0)
-    grad_tokens = d_hidden + norm_back(d_first, xhat_one, rstd_one, gain_one)
-    spread = lax.psum(
-        jnp.stack(
-            [grad_gain_one, grad_shift_one, grad_bout, grad_gain_two, grad_shift_two, grad_breduce]
-        ),
-        ("dp", "mp"),
-    )
-    ranks = lax.psum(jnp.concatenate([grad_bq, grad_bv, grad_bexpand]), "dp")
+    ranks = jnp.pad(jnp.concatenate([grad_bq, grad_bv, grad_bexpand]), (0, 2 * width))
+    ranks = ranks[: 2 * width].reshape(2, width)
+    gparts = attn_grads.astype(BF16).reshape(nd, part, -1)
+    grad_tokens, attn_owned, sums = exchange(
+        functools.partial(end_kernel, nz, nd),
+        3,
+        [(own_shape, F32), (gparts.shape[1:], F32), ((8, width), F32)],
+        [
+            landing[0],
+            pltpu.VMEM((nd - 1,) + gparts.shape[1:], BF16),
+            pltpu.VMEM((8, width), F32),
+            pltpu.VMEM((nz - 1, 8, width), F32),
+            pltpu.VMEM((8, width), F32),
+            pltpu.VMEM((nd - 1, 8, width), F32),
+        ]
+        + sems(2 * nz - 2)
+        + sems(2 * nd - 2),
+        d_first_part,
+        gparts,
+        tokens[0],
+        gain_one,
+        d_hidden,
+        vec,
+        ranks,
+    )
+    spread = sums[:6]
+    count = 2 * hrows + frows
+    ranks = sums[6:].reshape(-1)[: count * HD]
     me = lax.axis_index("dp")
     spread = lax.dynamic_slice_in_dim(spread, me * part, part, 1)
     ranks = lax.dynamic_slice_in_dim(ranks.reshape(-1, HD), me * hcols, hcols, 1)

time: 547 us -> 365 us (0.67); the launches traced: 538 us -> 364 us
  waiting for transfers between devices: 348 us -> 0.77 us
  Pallas kernels: 0 us -> 231 us
  blocking collectives: 62.6 us -> 0 us
  local copies, waits for them, and re-layouts: 25.1 us -> 34.7 us
    pallas_call x0 -> x4, Pallas kernels: none -> 231 us  [exchange(): pl.pallas_call(kernel, out_shape=[jax.ShapeDtypeStruct(*out) for out in o...]
    all_gather x4 -> x1, waiting for transfers between devices: 133 us -> 0.01 us  [gather_rows(): return lax.all_gather(v, 'mp', axis=0, tiled=True)]
    reduce_scatter x4 -> x1, waiting for transfers between devices: 131 us -> 0.01 us  [scatter_rows(): lax.psum_scatter(v.astype(BF16), 'mp', scatter_dimension=0, tiled=True)]
    psum x2 -> x0, blocking collectives: 62.6 us -> none  [the longest x1 39.4 us: local(): lax.psum(jnp.stack([grad_gain_one, grad_shift_one, grad_bout, grad_gain_t...]
    unnamed x14 -> x5, waiting for transfers between devices: 36.4 us -> 0.75 us
    all_gather x1, waiting for transfers between devices: 24.8 us -> 0.02 us  [local(): lax.all_gather(jnp.concatenate([w_expand, w_reduce.T], axis=1), 'dp', til...]
    all_gather x1 -> x0, waiting for transfers between devices: 22.4 us -> none  [local(): lax.all_gather(jnp.concatenate([w_query, w_key, w_value, w_out.T, columns...]
    convert_element_type x2, other arithmetic: 1.93 us -> 9.25 us  [attend_backward(): d_scores = (probs * (d_probs - inner)).astype(BF16)]
  transfers between devices with their start and end apart: 12 -> 4, of which waited for: 12 -> 0; matrix products, arithmetic and copies ran while one was open for 12% -> 21% of each run, Pallas kernels for 0% -> 44%
where the time goes in v2:
time: 365 us; the launch traced here: 364 us
  Pallas kernels  231 us (63%)
  matrix products  63.6 us (17%)
  local copies, waits for them, and re-layouts  34.7 us (10%)
  other arithmetic  19.6 us (5%)
  between operations  14.4 us (4%)
    pallas_call x4, Pallas kernels, exchange(): pl.pallas_call(kernel, out_shape=[jax.ShapeDtypeStruct(*out) for out in o...  231 us
    unnamed x90, local copies, waits for them, and re-layouts  17.3 us
    dot_general x4, matrix products, dot(): return jnp.dot(a, b, preferred_element_type=F32)  13.9 us
    dot_general x4, matrix products, dot_nt(): lax.dot_general(a, b, (((1,), (1,)), ((), ())), preferred_element_type=F32)  10.6 us
    convert_element_type x2, other arithmetic, attend_backward(): d_scores = (probs * (d_probs - inner)).astype(BF16)  9.25 us
    sub x2, matrix products, attend_forward(): expo = jnp.exp(scores - top)  9.05 us
    dot_general x2, matrix products, attend_backward(): jnp.einsum('qhd,khd->hqk', dhead[first:end], vhead[:end], preferred_eleme...  9.03 us
  transfers between devices with their start and end apart: 4, of which 0 were waited for; matrix products, arithmetic and copies ran while one was open for 21% of the time, Pallas kernels for 44%

profile of v2, /device:TPU:0, one launch (start us, length us, event | category | flops | bytes accessed | tf_op | source)
XLA Modules:
  0.0 363.9 jit_solution(1559711521394330406)
XLA Ops:
  7.2 1.7 pad_maximum_fusion.4
  17.4 33.5 %shard_map.306 = (bf16[4,256,768]{2,1,0:T(8,128)(2,1)S(1)}, bf16[8,96,896]{2,1,0:T(8,128)(2,1)S(1)}) custom-call(bf16[256,768]{1,0:T(8,128)(2,1)S(1)} %bitcast.179, bf16[96,896]{1,0:T(8,128)(2,1)S(1)} %concatenate.42.pack), custom_call_target="tpu_custom_call" | custom-call | flops 24999999488 | bytes 60000000 | tf_op jit(solution)/shard_map/pallas_call | solution.py:177
  56.7 1.8 iota_compare_fusion
  59.9 1.5 copy.92
  61.4 1.5 add.129
  62.9 1.7 copy.97
  64.6 4.1 %fusion.92 = (f32[3,512]{1,0:T(4,128)S(1)}, f32[3,512,512]{1,2,0:T(8,128)}) fusion(pred[512,512]{0,1:T(8,128)(4,1)} %iota_compare_fusion.1, bf16[512,3,64]{0,2,1:T(8,128)(2,1)} %bitcast.196, bf16[512,3,64]{0,2,1:T(8,128)(2,1)} %bitcast.198), kind=kOutput, calls=%fused_computation.147 | convolution fusion | flops 103809536 | bytes 3807232 | tf_op jit(solution)/shard_map/sub | solution.py:225
  68.7 2.3 convolution_convert_fusion.8
  71.1 4.9 %fusion.91 = (f32[3,512]{1,0:T(4,128)S(1)}, f32[3,512,1024]{2,1,0:T(8,128)}) fusion(pred[512,1024]{1,0:T(8,128)(4,1)S(1)} %copy-done.17, bf16[512,3,64]{0,2,1:T(8,128)(2,1)S(1)} %bitcast.191, bf16[1024,3,64]{0,2,1:T(8,128)(2,1)S(1)} %bitcast.189), kind=kOutput, calls=%fused_computation.146 | convolution fusion | flops 207619072 | bytes 7411712 | tf_op jit(solution)/shard_map/sub | solution.py:225
  76.0 4.0 %fusion.52 = bf16[3,64,512]{2,1,0:T(8,128)(2,1)S(1)} fusion(bf16[1024,3,64]{0,2,1:T(8,128)(2,1)S(1)} %bitcast.205, f32[3,512,1024]{2,1,0:T(8,128)} %get-tuple-element.191, f32[3,512]{1,0:T(4,128)S(1)} %get-tuple-element.190), kind=kOutput, calls=%fused_computation.81 | convolution fusion | flops 204570624 | bytes 6887424 | tf_op jit(solution)/shard_map/hqk,khd->qhd/dot_general | solution.py:228
  80.9 71.0 %shard_map.307 = (bf16[4,256,768]{2,1,0:T(8,128)(2,1)S(1)}, f32[256,768]{1,0:T(8,128)S(1)}) custom-call(bf16[4,256,768]{2,1,0:T(8,128)(2,1)S(1)} %bitcast.170, bf16[256,768]{1,0:T(8,128)(2,1)S(1)} %bitcast.180, f32[1,768]{1,0:T(1,128)S(1)} %get-tuple-element.171.bias, f32[1,768]{1,0:T(1,128)S(1)} %get-tuple-element.170.gain, ...), custom_call_target="tpu_custom_call" | custom-call | flops 24999999488 | bytes 60000000 | tf_op jit(solution)/shard_map/pallas_call | solution.py:177
  152.0 4.4 %fusion.58 = f32[1024,768]{1,0:T(8,128)} fusion(bf16[1024,768]{1,0:T(8,128)(2,1)S(1)} %bitcast.183, bf16[768,1536]{1,0:T(8,128)(2,1)} %all-gather.4.cloned.1.call-done), kind=kOutput, calls=%fused_computation.87 | convolution fusion | flops 1207959552 | bytes 5898240 | tf_op jit(solution)/shard_map/dot_general | solution.py:35
  156.4 6.2 %convert_reduce_fusion = (f32[768]{0:T(1024)S(1)}, bf16[1024,768]{1,0:T(8,128)(2,1)S(1)}) fusion(bf16[768,1536]{1,0:T(8,128)(2,1)} %all-gather.4.cloned.1.call-done, bf16[1,1024,768]{2,1,0:T(8,128)(2,1)} %all-gather.6.cloned.1.call-done, f32[1024,768]{1,0:T(8,128)} %fusion.58, f32[768]{0:T(1024)S(1)} %copy-done.33), kind=kOutput, calls=%fused_computation.27 | convolution fusion | flops 1229192448 | bytes 7477248 | tf_op jit(solution)/shard_map/dot_general | solution.py:35
  162.6 1.5 convolution_convert_fusion.4
  164.3 1.7 convolution_convert_fusion.1
  166.0 70.1 %shard_map.308 = (bf16[4,256,768]{2,1,0:T(8,128)(2,1)S(1)}, f32[256,768]{1,0:T(8,128)S(1)}, f32[4,768]{1,0:T(4,128)S(1)}) custom-call(bf16[4,256,768]{2,1,0:T(8,128)(2,1)S(1)} %bitcast.185, f32[256,768]{1,0:T(8,128)S(1)} %get-tuple-element.93.hidden, bf16[256,768]{1,0:T(8,128)(2,1)S(1)} %bitcast.177, f32[1,768]{1,0:T(1,128)S(1)} %get-tuple-element.170.gain), custom_call_target="tpu_custom_call" | custom-call | flops 24999999488 | bytes 60000000 | tf_op jit(solution)/shard_map/pallas_call | solution.py:177
  236.1 2.2 convolution_convert_fusion.7
  240.4 2.3 multiply_reduce_fusion.1
  243.9 1.9 fusion.33
  245.8 1.6 pad_maximum_fusion
  247.5 4.3 %copy.110 = bf16[768,1536]{1,0:T(8,128)(2,1)} copy(bf16[768,1536]{0,1:T(8,128)(2,1)} %pad_maximum_fusion) | data formatting | bytes 4718592
  251.7 5.5 %convolution_convert_fusion.2 = bf16[1024,768]{1,0:T(8,128)(2,1)} fusion(bf16[768,1536]{1,0:T(8,128)(2,1)} %all-gather.4.cloned.1.call-done, f32[1024,768]{1,0:T(8,128)} %fusion.58, f32[768]{0:T(1024)S(1)} %copy-done.33), kind=kOutput, calls=%fused_computation.44 | convolution fusion | flops 1216610304 | bytes 5901312 | tf_op jit(solution)/shard_map/dot_general | solution.py:43
  257.4 6.8 %multiply_reduce_fusion = (f32[3,512]{1,0:T(4,128)S(1)}, f32[3,512,1024]{2,1,0:T(8,128)}) fusion(f32[3,512,1024]{2,1,0:T(8,128)} %get-tuple-element.191, f32[3,512]{1,0:T(4,128)S(1)} %copy-done.30, bf16[512,3,64]{0,2,1:T(8,128)(2,1)} %bitcast.215, bf16[1024,3,64]{0,2,1:T(8,128)(2,1)S(1)} %bitcast.206), kind=kOutput, calls=%fused_computation.3 | convolution fusion | flops 206043648 | bytes 13185024 | tf_op jit(solution)/shard_map/qhd,khd->hqk/dot_general | solution.py:250
  264.2 4.4 %convert_reduce_fusion.2 = (f32[3,64]{1,0:T(4,128)S(1)}, bf16[1024,3,64]{0,2,1:T(8,128)(2,1)}) fusion(bf16[512,3,64]{0,2,1:T(8,128)(2,1)S(1)} %bitcast.216, f32[3,512,1024]{2,1,0:T(8,128)} %get-tuple-element.191, f32[3,512]{1,0:T(4,128)S(1)} %copy-done.30, f32[512,3,64]{0,2,1:T(8,128)S(1)} %copy-done.38), kind=kOutput, calls=%fused_computation.91 | convolution fusion | flops 205258560 | bytes 7281408 | tf_op jit(solution)/shard_map/hqk,qhd->khd/dot_general | solution.py:264
  268.6 1.8 copy.98
  270.5 4.0 %multiply_convert_fusion.1 = bf16[3,512,512]{1,2,0:T(8,128)(2,1)S(1)} fusion(f32[3,512,512]{1,2,0:T(8,128)} %get-tuple-element.197, f32[3,512]{1,0:T(4,128)S(1)} %get-tuple-element.196, f32[3,512,512]{1,2,0:T(8,128)} %get-tuple-element.193, f32[3,512]{1,0:T(4,128)S(1)} %copy-done.32), kind=kLoop, calls=%fused_computation.28 | loop fusion | flops 3145728 | bytes 7876608 | tf_op jit(solution)/shard_map/convert_element_type | solution.py:254
  274.9 5.2 %multiply_convert_fusion = bf16[3,512,1024]{2,1,0:T(8,128)(2,1)S(1)} fusion(f32[3,512,1024]{2,1,0:T(8,128)} %get-tuple-element.195, f32[3,512]{1,0:T(4,128)S(1)} %get-tuple-element.194, f32[3,512,1024]{2,1,0:T(8,128)} %get-tuple-element.191, f32[3,512]{1,0:T(4,128)S(1)} %copy-done.30), kind=kLoop, calls=%fused_computation.2 | loop fusion | flops 6291456 | bytes 15740928 | tf_op jit(solution)/shard_map/convert_element_type | solution.py:254
  285.0 2.6 convolution_convert_fusion
  287.6 1.4 convolution_convert_fusion.5
  289.4 1.4 copy-done.5
  291.9 56.0 %shard_map.309 = (f32[256,768]{1,0:T(8,128)S(1)}, f32[96,768]{1,0:T(8,128)S(1)}, f32[8,768]{1,0:T(8,128)S(1)}) custom-call(bf16[4,256,768]{2,1,0:T(8,128)(2,1)S(1)} %bitcast.182, bf16[8,96,768]{2,1,0:T(8,128)(2,1)S(1)} %pad_maximum_fusion.2.grads, bf16[256,768]{1,0:T(8,128)(2,1)S(1)} %bitcast.181, f32[1,768]{1,0:T(1,128)S(1)} %get-tuple-element.169.gain, ...), custom_call_target="tpu_custom_call" | custom-call | flops 24999999488 | bytes 60000000 | tf_op jit(solution)/shard_map/pallas_call | solution.py:177
  351.6 1.8 fusion.66
  (157 shorter events, 34.3 us)
Async XLA Ops:
  7.2 144.8 %all-gather.4.cloned.1.call-start = ((), (), s32[]{:S(2)}) async-start(), calls=%async_computation.2 | async-start | bytes 2654208 | tf_op jit(solution)/shard_map/all_gather | solution.py:326
  9.0 147.4 %all-gather.6.cloned.1.call-start = ((), (), s32[]{:S(2)}) async-start(), calls=%async_computation.4 | async-start | bytes 1966080 | tf_op jit(solution)/shard_map/all_gather | solution.py:197
  9.7 341.9 %reduce-scatter.5.cloned.1.call-start = ((), (), s32[]{:S(2)}) async-start(), calls=%async_computation.3 | async-start | bytes 1966080 | tf_op jit(solution)/shard_map/reduce_scatter | solution.py:201
  50.9 29.2 %copy-start = (bf16[8,96,896]{2,1,0:T(8,128)(2,1)}, bf16[8,96,896]{2,1,0:T(8,128)(2,1)S(1)}, u32[]{:S(2)}) copy-start(bf16[8,96,896]{2,1,0:T(8,128)(2,1)S(1)} %get-tuple-element.92) | copy-start | bytes 4128772
  55.9 7.0 %copy-start.9 = (bf16[1024,768]{1,0:T(8,128)(2,1)S(1)}, bf16[1024,768]{1,0:T(8,128)(2,1)}, u32[]{:S(2)}) copy-start(bf16[1024,768]{1,0:T(8,128)(2,1)} %copy-done.8) | copy-start | bytes 4718596
  56.7 14.4 %copy-start.13 = (bf16[1024,192]{0,1:T(8,128)(2,1)}, bf16[1024,192]{0,1:T(8,128)(2,1)S(1)}, u32[]{:S(2)}) copy-start(bf16[1024,192]{0,1:T(8,128)(2,1)S(1)} %get-tuple-element.161) | copy-start | bytes 1179652
  64.6 4.1 %copy-start.23 = (bf16[512,192]{0,1:T(8,128)(2,1)S(1)}, bf16[512,192]{0,1:T(8,128)(2,1)}, u32[]{:S(2)}) copy-start(bf16[512,192]{0,1:T(8,128)(2,1)} %get-tuple-element.160) | copy-start | bytes 589828
  68.7 2.4 copy-start.31
  68.7 2.4 copy-start.17
  71.0 9.1 %copy-start.21 = (bf16[3,64,512]{2,1,0:T(8,128)(2,1)}, bf16[3,64,512]{2,1,0:T(8,128)(2,1)S(1)}, u32[]{:S(2)}) copy-start(bf16[3,64,512]{2,1,0:T(8,128)(2,1)S(1)} %convolution_convert_fusion.8) | copy-start | bytes 589828
  71.1 5.0 %copy-start.19 = (bf16[1024,192]{0,1:T(8,128)(2,1)S(1)}, bf16[1024,192]{0,1:T(8,128)(2,1)}, u32[]{:S(2)}) copy-start(bf16[1024,192]{0,1:T(8,128)(2,1)} %get-tuple-element.162) | copy-start | bytes 1179652
  76.0 4.0 %copy-start.29 = (f32[3,512]{1,0:T(4,128)}, f32[3,512]{1,0:T(4,128)S(1)}, u32[]{:S(2)}) copy-start(f32[3,512]{1,0:T(4,128)S(1)} %get-tuple-element.190) | copy-start | bytes 18436
  76.0 4.9 %copy-start.4 = (bf16[1,256,768]{2,1,0:T(8,128)(2,1)S(1)}, bf16[1,256,768]{2,1,0:T(8,128)(2,1)}, u32[]{:S(2)}) copy-start(bf16[1,256,768]{2,1,0:T(8,128)(2,1)} %param.29) | copy-start | bytes 1179652
  152.0 4.4 %copy-start.33 = (f32[768]{0:T(1024)S(1)}, f32[768]{0:T(1024)}, u32[]{:S(2)}) copy-start(f32[768]{0:T(1024)} %add.129) | copy-start | bytes 9220
  162.6 1.7 copy-start.34
  164.3 1.7 copy-start.2
  166.0 73.1 %copy-start.32 = (f32[3,512]{1,0:T(4,128)S(1)}, f32[3,512]{1,0:T(4,128)}, u32[]{:S(2)}) copy-start(f32[3,512]{1,0:T(4,128)} %copy-done.31) | copy-start | bytes 18436
  236.1 4.3 %copy-start.6 = (f32[256,768]{1,0:T(8,128)}, f32[256,768]{1,0:T(8,128)S(1)}, u32[]{:S(2)}) copy-start(f32[256,768]{1,0:T(8,128)S(1)} %get-tuple-element.96.d_hidden) | copy-start | bytes 2359300
  236.1 2.9 copy-start.10
  240.4 2.3 copy-start.35
  240.4 3.5 copy-start.37
  251.7 5.6 %copy-start.20 = (bf16[1024,192]{0,1:T(8,128)(2,1)S(1)}, bf16[1024,192]{0,1:T(8,128)(2,1)}, u32[]{:S(2)}) copy-start(bf16[1024,192]{0,1:T(8,128)(2,1)} %get-tuple-element.162) | copy-start | bytes 1179652
  251.7 5.6 %copy-start.30 = (f32[3,512]{1,0:T(4,128)S(1)}, f32[3,512]{1,0:T(4,128)}, u32[]{:S(2)}) copy-start(f32[3,512]{1,0:T(4,128)} %copy-done.29) | copy-start | bytes 18436
  257.3 96.1 %reduce-scatter.7.cloned.1.call-start = ((), (), s32[]{:S(2)}) async-start(), calls=%async_computation.5 | async-start | bytes 2654208
  257.4 6.8 %copy-start.27 = (bf16[512,192]{0,1:T(8,128)(2,1)S(1)}, bf16[512,192]{0,1:T(8,128)(2,1)}, u32[]{:S(2)}) copy-start(bf16[512,192]{0,1:T(8,128)(2,1)} %get-tuple-element.164) | copy-start | bytes 589828
  257.4 6.8 %copy-start.38 = (f32[512,3,64]{0,2,1:T(8,128)S(1)}, f32[512,3,64]{0,2,1:T(8,128)}, u32[]{:S(2)}) copy-start(f32[512,3,64]{0,2,1:T(8,128)} %convolution_bitcast_fusion) | copy-start | bytes 1179652
  270.5 4.0 %copy-start.16 = (bf16[512,192]{0,1:T(8,128)(2,1)S(1)}, bf16[512,192]{0,1:T(8,128)(2,1)}, u32[]{:S(2)}) copy-start(bf16[512,192]{0,1:T(8,128)(2,1)} %get-tuple-element.157) | copy-start | bytes 589828
  274.9 5.3 %copy-start.14 = (bf16[1024,192]{0,1:T(8,128)(2,1)S(1)}, bf16[1024,192]{0,1:T(8,128)(2,1)}, u32[]{:S(2)}) copy-start(bf16[1024,192]{0,1:T(8,128)(2,1)} %copy-done.13) | copy-start | bytes 1179652
  280.2 2.8 copy-start.15
  285.0 2.6 copy-start.11
  287.6 1.6 copy-start.18
  291.9 59.6 %copy-start.28 = (f32[768]{0:T(1024)S(1)}, f32[768]{0:T(1024)}, u32[]{:S(2)}) copy-start(f32[768]{0:T(1024)} %get-tuple-element.176) | copy-start | bytes 9220
  (11 other events, 14.1 us)
Sparse Core Ops, SparseCore 0:
  10.5 41.2 all-gather.3
  53.4 37.0 all-gather.5
  257.4 43.8 reduce-scatter.4
  304.5 42.7 reduce-scatter.6
